TPU v7x, 32 devices: a whole 2x2x4 slice. The times are simulated.
32 devices in a mesh: wide: 8 (over z, x), narrow: 4 (over y, core).
Axes of the slice: x: 2, y: 2, z: 4, core: 2. Of those that a mesh axis runs over, the one named last changes fastest.
Arguments:
- tokens: bfloat16 [32768, 512], P(('wide', 'narrow')), may hold values from -11 to 11
- cotangent: float32 [32768, 512], P(('wide', 'narrow')), may hold values from -6 to 6
- cells: int32 [32, 1024], P(('wide', 'narrow')), may hold values from 0 to 3, never falling along the last dimension, each value on 1 to 512 neighbouring positions
- present: int32 [32, 1024], P(('wide', 'narrow')), may hold values 0 or 1
- generate: int32 [32, 1024], P(('wide', 'narrow')), may hold values 0 or 1
- w_qkv: float32 [512, 1536], P('narrow'), may hold values from -0.25 to 0.25
- w_out: float32 [512, 512], P('narrow'), may hold values from -1 to 1
- w_up: float32 [512, 512], P('narrow'), may hold values from -0.25 to 0.25
- w_down: float32 [512, 512], P('narrow'), may hold values from -0.25 to 0.25
- vectors: float32 [9, 512], P(None, 'narrow'), may hold values from -1.5 to 3.2
- m_qkv: float32 [512, 1536], P('narrow'), may hold values from -2 to 2
- m_out: float32 [512, 512], P('narrow'), may hold values from -2 to 2
- m_up: float32 [512, 512], P('narrow'), may hold values from -2 to 2
- m_down: float32 [512, 512], P('narrow'), may hold values from -2 to 2
- m_vec: float32 [9, 512], P(None, 'narrow'), may hold values from -4 to 4
- v_qkv: float32 [512, 1536], P('narrow'), may hold values from 0.010386238 to 0.1661798
- v_out: float32 [512, 512], P('narrow'), may hold values from 0.010386238 to 0.1661798
- v_up: float32 [512, 512], P('narrow'), may hold values from 0.010386238 to 0.1661798
- v_down: float32 [512, 512], P('narrow'), may hold values from 0.010386238 to 0.1661798
- v_vec: float32 [9, 512], P(None, 'narrow'), may hold values from 0.09347615 to 1.4956183
Outputs:
- mixed: bfloat16 [32768, 512], P(('wide', 'narrow'))
- input_grad: float32 [32768, 512], P(('wide', 'narrow'))
- grad_norm: float32 [], replicated
- new_qkv: float32 [512, 1536], P('narrow')
- new_out: float32 [512, 512], P('narrow')
- new_up: float32 [512, 512], P('narrow')
- new_down: float32 [512, 512], P('narrow')
- new_vectors: float32 [9, 512], P(None, 'narrow')
- first_qkv: float32 [512, 1536], P('narrow')
- first_out: float32 [512, 512], P('narrow')
- first_up: float32 [512, 512], P('narrow')
- first_down: float32 [512, 512], P('narrow')
- first_vec: float32 [9, 512], P(None, 'narrow')
- second_qkv: float32 [512, 1536], P('narrow')
- second_out: float32 [512, 512], P('narrow')
- second_up: float32 [512, 512], P('narrow')
- second_down: float32 [512, 512], P('narrow')
- second_vec: float32 [9, 512], P(None, 'narrow')
- copy_qkv: bfloat16 [512, 1536], P('narrow')
- copy_out: bfloat16 [512, 512], P('narrow')
- copy_up: bfloat16 [512, 512], P('narrow')
- copy_down: bfloat16 [512, 512], P('narrow')
- copy_vec: bfloat16 [9, 512], P(None, 'narrow')
Inputs may be any that keep to these rules, and one draw needn't show every extreme that they name: `cells`: within a row cell numbers never fall; each cell holds 1 to 512 tokens, one exactly that many.
All inputs are finite; a program needn't handle non-finite values. No bound on the sum of `present` or of `generate` on one device may be relied on, other than what follows from the above.
Results may differ from a plain program's by a relative error of at most 0.012.
Values may be sent and summed in bfloat16 or wider, within the bound.
No kernel may reach another device: no remote copies, remote signals or barrier semaphores. Data moves between devices by JAX's collectives and lax.ppermute only.
A program may use at most 192 MiB of HBM per device.

v0:
```python
import functools
import math

import jax
import jax.numpy as jnp
from jax import lax
from jax.experimental import pallas as pl
from jax.experimental.pallas import tpu as pltpu
from jax.sharding import PartitionSpec as P

D = 512
HEADS = 8
HEAD_DIM = 64
PAIR = 2 * HEAD_DIM
PAIRS = HEADS // 2
TRIO = 3 * PAIR
TOK_DEV = 1024
QT = 256
HALF = TOK_DEV // 2
TILES = 1
MT = 512
STEP = 10
NORM_EPS = 1e-05
ADAM_EPS = 1e-08
MASKED = -1e30
HIDDEN = 16
BF = jnp.bfloat16
F32 = jnp.float32
MIB = 1024 * 1024
GROUP = 2
HW = GROUP * TRIO
FIRST = 1
LATE = (PAIRS - FIRST) * TRIO
FORWARD_MIB, MIDDLE_MIB, BACKWARD_MIB = 12, 18, 20

NN = (((1,), (0,)), ((), ()))
NT = (((1,), (1,)), ((), ()))
TN = (((0,), (0,)), ((), ()))


def dot(a, b, dims):
    return lax.dot_general(a, b, dims, preferred_element_type=F32)


def params(mib=8):
    return pltpu.CompilerParams(vmem_limit_bytes=mib * MIB)


def sds(shape, dtype):
    return jax.ShapeDtypeStruct(shape, dtype)


SMEM = pl.BlockSpec(memory_space=pltpu.SMEM)
VM = pl.BlockSpec(memory_space=pltpu.VMEM)
ANY = pl.BlockSpec(memory_space=pl.ANY)
HBM = pl.BlockSpec(memory_space=pltpu.HBM)


def whole(shape):
    return pl.BlockSpec(shape, lambda i: (0,) * len(shape))


def cost(flops, moved, exps=0):
    return pl.CostEstimate(flops=int(flops), bytes_accessed=int(moved), transcendentals=int(exps))


def fetch(pairs, sems):
    copies = [
        pltpu.make_async_copy(source, target, sems.at[number])
        for number, (source, target) in enumerate(pairs)
    ]
    for copy in copies:
        copy.start()
    return copies


def trio_columns(base):
    return [
        (local * TRIO + t * PAIR, t * D + (base + local) * PAIR)
        for local in range(GROUP)
        for t in range(3)
    ]


def pack_first_kernel(w_hbm, vec_hbm, out_ref, w_ref, vec_ref, sems):
    rows, vec_cols = w_hbm.shape[0], vec_hbm.shape[1]
    width = GROUP * PAIR
    copies = fetch(
        [(w_hbm.at[:, t * D : t * D + width], w_ref.at[t]) for t in range(3)] + [(vec_hbm, vec_ref)], sems
    )
    for copy in copies:
        copy.wait()
    for local in range(GROUP):
        for t in range(3):
            target = local * TRIO + t * PAIR
            out_ref[:rows, target : target + PAIR] = w_ref[t, :, local * PAIR : (local + 1) * PAIR].astype(BF)
    out_ref[rows:, :] = jnp.zeros((16, HW), BF)
    vec = jnp.concatenate([vec_ref[...], jnp.zeros((7, vec_cols), F32)], 0)
    out_ref[rows:, :vec_cols] = vec.astype(BF)


def pack_first(w_qkv, vectors):
    rows = w_qkv.shape[0]
    return pl.pallas_call(
        pack_first_kernel,
        in_specs=[HBM, HBM],
        out_specs=VM,
        out_shape=sds((rows + 16, HW), BF),
        scratch_shapes=[
            pltpu.VMEM((3, rows, GROUP * PAIR), F32),
            pltpu.VMEM(vectors.shape, F32),
            pltpu.SemaphoreType.DMA((4,)),
        ],
        compiler_params=params(60),
        name="pack_first",
    )(w_qkv, vectors)


def pack_second_kernel(w_ref, w_out_ref, w_up_ref, w_down_ref, *refs):
    second_ref, rest_ref = refs[-2:]
    for target, source in trio_columns(GROUP):
        second_ref[:, target : target + PAIR] = w_ref[:, source : source + PAIR].astype(BF)
    rest_ref[:, :D] = w_out_ref[...].astype(BF)
    rest_ref[:, D : 2 * D] = w_up_ref[...].astype(BF)
    rest_ref[:, 2 * D :] = w_down_ref[...].astype(BF)


def pick(piece, lead, rows):
    return piece[rows, :] if lead is None else piece[lead, rows, :]


def assemble(order, pieces, place, w_full):
    rows = D // len(order)
    for number, (piece, lead, mask) in enumerate(order):
        at = number if mask is None else jnp.bitwise_xor(place[0], mask)
        w_full[pl.ds(pl.multiple_of(at * rows, rows), rows), :] = pick(
            pieces[piece], lead, slice(0, rows)
        )


def turn_rows(source, start, write):
    blocks = source.shape[0] // 8
    whole_blocks, rest = start >> 3, start & 7
    inside = lax.broadcasted_iota(jnp.int32, (8, source.shape[1]), 0) < 8 - rest

    def rolled(block):
        at = pl.multiple_of(((block + whole_blocks) & (blocks - 1)) * 8, 8)
        return pltpu.roll(source[pl.ds(at, 8), :], (8 - rest) & 7, 0)

    def step(i, first):
        second, third = rolled(2 * i + 1), rolled(2 * i + 2)
        write(i, jnp.where(inside, first, second), jnp.where(inside, second, third))
        return third

    lax.fori_loop(0, blocks // 2, step, rolled(0), unroll=8)


def write_into(out):
    def write(i, upper, lower):
        at = pl.multiple_of(i * 16, 16)
        out[pl.ds(at, 16), :] = jnp.concatenate([upper, lower], 0).astype(out.dtype)

    return write


def turn_tokens_kernel(tokens, coded, *refs):
    tokens_out, turned_out, cells_out, start_out, wide_tokens = refs[-5:]
    seen = coded[...] < HIDDEN
    cell = jnp.where(seen, coded[...], coded[...] - HIDDEN)
    start = jnp.int32(TOK_DEV)
    for c in range(4):
        size = jnp.sum((cell == c).astype(jnp.int32))
        first = jnp.sum((cell < c).astype(jnp.int32))
        start = jnp.where(size == HALF, jnp.minimum(start, first), start)
    start_out[0] = start
    shift = jnp.where(start == 0, 0, TOK_DEV - start)
    row = lax.broadcasted_iota(jnp.int32, (8, TOK_DEV), 0)
    cells_out[...] = pltpu.roll(jnp.where((row == 0) | seen, cell, -1), shift, 1)
    wide_tokens[...] = tokens[...].astype(F32)
    turn_rows(wide_tokens, start, write_into(tokens_out))
    turned_out[...] = tokens_out[...].T


def turn_tokens(tokens, coded):
    return pl.pallas_call(
        turn_tokens_kernel,
        in_specs=[VM, VM],
        out_specs=[VM] * 3 + [SMEM],
        out_shape=[
            sds((TOK_DEV, D), BF),
            sds((D, TOK_DEV), BF),
            sds((8, TOK_DEV), jnp.int32),
            sds((1,), jnp.int32),
        ],
        scratch_shapes=[pltpu.VMEM((TOK_DEV, D), F32)],
        compiler_params=params(),
        cost_estimate=cost(1e7, 3e6),
        name="turn_tokens",
    )(tokens, coded)


def turn_cotangent_kernel(start, cot_ref, *refs):
    turn_rows(cot_ref, start[0], write_into(refs[-1]))


def turn_cotangent(start, cot, later):
    return pl.pallas_call(
        turn_cotangent_kernel,
        in_specs=[SMEM, VM] + [ANY] * len(later),
        out_specs=VM,
        out_shape=sds((TOK_DEV, D), F32),
        compiler_params=params(),
        cost_estimate=cost(1e7, 4e6),
        name="turn_cotangent",
    )(start, cot, *later)


def turn_back_kernel(start, source, *refs):
    turned, wide_source = refs[-2:]
    back = (TOK_DEV - start[0]) & (TOK_DEV - 1)
    if source.dtype == F32:
        turn_rows(source, back, write_into(turned))
    else:
        wide_source[...] = source[...].astype(F32)
        turn_rows(wide_source, back, write_into(turned))


def turn_back(start, value, later):
    scratch = (8, PAIR) if value.dtype == F32 else value.shape
    return pl.pallas_call(
        turn_back_kernel,
        in_specs=[SMEM, VM] + [ANY] * len(later),
        out_specs=VM,
        out_shape=sds(value.shape, value.dtype),
        scratch_shapes=[pltpu.VMEM(scratch, F32)],
        compiler_params=params(),
        cost_estimate=cost(1, 1),
        name="turn_back",
    )(start, value, *later)


def make_bias(cells_ref, bias):
    for half in range(2):
        mine = slice(half * HALF, (half + 1) * HALF)
        number = lax.broadcasted_iota(jnp.int32, (16, HALF), 0)
        of_key = jnp.where(cells_ref[1:2, mine] == number, 1.0, 0.0).astype(BF)
        of_query = jnp.where(cells_ref[0:1, mine] == number, 1.0, 0.0).astype(BF)
        keys = lax.broadcasted_iota(jnp.int32, (HALF, HALF), 0)
        queries = lax.broadcasted_iota(jnp.int32, (HALF, HALF), 1)
        seen = (dot(of_key, of_query, TN) > 0.5) | (keys == queries)
        bias[mine, :] = jnp.where(seen, 0.0, MASKED).astype(BF)


def column_of(row):
    eye = lax.broadcasted_iota(jnp.int32, (PAIR, PAIR), 0) == lax.broadcasted_iota(
        jnp.int32, (PAIR, PAIR), 1
    )
    return jnp.sum(jnp.where(eye, row, 0.0), 1, keepdims=True)


def both_heads(pair_t):
    zero = jnp.zeros((HEAD_DIM, pair_t.shape[1]), pair_t.dtype)
    return jnp.concatenate(
        [
            jnp.concatenate([pair_t[:HEAD_DIM], zero], 0),
            jnp.concatenate([zero, pair_t[HEAD_DIM:]], 0),
        ],
        1,
    )


def forward_kernel(order, n_pieces, base, *refs):
    place, tokens, tokens_t, bias, vec_in = refs[:5]
    pieces = refs[5 : 5 + n_pieces]
    att_out, lse_out, krow_out, vrow_out, qt_out, kt_out, w_full, vec_full, tokens_out = refs[
        5 + n_pieces : 14 + n_pieces
    ]
    if base == 0:
        make_bias(bias, refs[-1])
        bias = refs[-1]
    assemble(order, pieces, place, w_full)
    if vec_in.shape[1] == D:
        vec_full[...] = vec_in[...].astype(F32)
    else:
        rows = D // len(order)
        for piece, lead, mask in order:
            at = pl.multiple_of(jnp.bitwise_xor(place[0], mask) * rows, rows)
            vec_full[:, pl.ds(at, rows)] = pick(pieces[piece], lead, slice(rows, rows + 16))[
                :, :rows
            ].astype(F32)
    x = tokens[...]
    tokens_out[...] = x
    halves = [slice(0, HALF), slice(HALF, TOK_DEV)]
    chains = []
    for local in range(GROUP):
        lane = slice((base + local) * PAIR, (base + local + 1) * PAIR)
        w = w_full[:, local * TRIO : (local + 1) * TRIO]
        b_q = vec_full[0:1, lane]
        b_v = vec_full[1:2, lane]
        trio = dot(w, tokens_t[...], TN)
        rows = dot(x, w[:, PAIR:], NN)
        here = slice(local * PAIR, (local + 1) * PAIR)
        q_t = ((trio[:PAIR] + column_of(b_q)) * (HEAD_DIM**-0.5)).astype(BF)
        v_t = (trio[2 * PAIR :] + column_of(b_v)).astype(BF)
        k_row = rows[:, :PAIR].astype(BF)
        krow_out[local] = k_row
        vrow_out[local] = (rows[:, PAIR:] + b_v).astype(BF)
        qt_out[here, :] = q_t
        kt_out[here, :] = trio[PAIR : 2 * PAIR].astype(BF)
        chains += [(local, mine, q_t, v_t, k_row) for mine in halves]

    def scores(chain):
        local, mine, q_t, v_t, k_row = chain
        return dot(k_row[mine], both_heads(q_t[:, mine]), NN)

    ahead = scores(chains[0])
    for number, (local, mine, q_t, v_t, k_row) in enumerate(chains):
        s = ahead
        if number + 1 < len(chains):
            ahead = scores(chains[number + 1])
        mask = bias[mine, :].astype(F32)
        s = s + jnp.concatenate([mask, mask], 1)
        top = jnp.max(s, 0, keepdims=True)
        e = jnp.exp(s - top)
        total = jnp.sum(e, 0, keepdims=True)
        lse = top + jnp.log(total)
        e_low = e.astype(BF)
        for h in range(2):
            cols = slice(h * HALF, (h + 1) * HALF)
            head = slice(h * HEAD_DIM, (h + 1) * HEAD_DIM)
            o = dot(v_t[head, mine], e_low[:, cols], NN)
            at = local * PAIR + h * HEAD_DIM
            att_out[at : at + HEAD_DIM, mine] = (o / total[:, cols]).astype(BF)
            lse_out[local, h : h + 1, mine] = lse[:, cols]


def forward_attention(base, place, tokens, tokens_t, cells, vec, pieces, order):
    mask = [] if base else [sds((TOK_DEV, HALF), BF)]
    wide_t, tall = sds((GROUP * PAIR, TOK_DEV), BF), sds((GROUP, TOK_DEV, PAIR), BF)
    return pl.pallas_call(
        functools.partial(forward_kernel, order, len(pieces), base),
        in_specs=[SMEM] + [VM] * (4 + len(pieces)),
        out_specs=[VM] * (9 + len(mask)),
        out_shape=[
            wide_t, sds((GROUP, 8, TOK_DEV), F32), tall, tall, wide_t, wide_t, sds((D, HW), BF), sds((16, D), F32),
            sds((TOK_DEV, D), BF),
        ]
        + mask,
        compiler_params=params(FORWARD_MIB),
        cost_estimate=cost(1, 1),
        name="forward_attention",
    )(place, tokens, tokens_t, cells, vec, *pieces)


def normalize(value):
    center = value - jnp.mean(value, -1, keepdims=True)
    inverse = lax.rsqrt(jnp.mean(center * center, -1, keepdims=True) + NORM_EPS)
    return center * inverse, inverse


def normalize_back(grad, normal, inverse):
    return inverse * (
        grad
        - jnp.mean(grad, -1, keepdims=True)
        - normal * jnp.mean(grad * normal, -1, keepdims=True)
    )


def column_sum(value):
    return jnp.sum(value, 0, keepdims=True)


def row_sources(place, n_shards, stages):
    if not stages:
        return [(0, 0, D)]
    rows = D // n_shards
    piece = D >> len(stages)
    found = []
    for block in range(1 << len(stages)):
        masks = {"narrow": 0, "wide": 0}
        for number, (axis, mask) in enumerate(stages):
            if block >> (len(stages) - 1 - number) & 1:
                masks[axis] |= mask
        source = jnp.bitwise_xor(place[0], masks["narrow"]) * rows
        if piece < rows:
            source = source + jnp.bitwise_xor(place[1], masks["wide"]) * piece
        found.append((block * piece, pl.multiple_of(source, piece), piece))
    return found


def store_rows(outs, place, n_shards, stages, matrix, cols):
    height = outs[0].shape[0]
    for target, source, rows in row_sources(place, n_shards, stages):
        out = outs[target // height]
        at = target % height
        out[at : at + rows, cols] = matrix[pl.ds(source, rows), :].astype(BF)


def gelu_parts(value):
    density = jnp.exp(-0.5 * value * value)
    t = 1.0 / (1.0 + (0.3275911 / math.sqrt(2.0)) * jnp.abs(value))
    poly = 1.061405429
    for factor in (-1.453152027, 1.421413741, -0.284496736, 0.254829592):
        poly = poly * t + factor
    tail = 0.5 * poly * t * density
    return jnp.where(value >= 0.0, 1.0 - tail, tail), value * density * (1.0 / math.sqrt(2.0 * math.pi))


def middle_kernel(order, n_pieces, *refs):
    place, tokens, cot_ref, att_a, att_b, vec_ref = refs[:6]
    pieces = refs[6 : 6 + n_pieces]
    mixed_out, dh1_out, datt_out, vec_out = refs[6 + n_pieces : 10 + n_pieces]
    first_all, hidden_all, branch_all, pre_all, down_all = refs[10 + n_pieces : 15 + n_pieces]
    w_full, sums = refs[15 + n_pieces :]
    step = pl.program_id(0)

    @pl.when(step == 0)
    def _():
        assemble(order, pieces, place, w_full)
        sums[...] = jnp.zeros_like(sums)

    w_out, w_up, w_down = w_full[:, :D], w_full[:, D : 2 * D], w_full[:, 2 * D :]

    def vec(row):
        return vec_ref[row : row + 1, :]

    def tile(number):
        at = pl.ds(pl.multiple_of(step * (TILES * MT) + number * MT, MT), MT)
        att_t = jnp.concatenate([att_a[:, at], att_b[:, at]], 0)
        branch = dot(att_t, w_out, TN)
        yield
        normal_1, inverse_1 = normalize(tokens[at, :].astype(F32) + (branch + vec(2)))
        first = normal_1 * vec(5) + vec(6)
        first_low = first.astype(BF)
        first_all[at, :] = first_low
        pre = dot(first_low, w_up, NN)
        yield
        pre = pre + vec(3)
        cdf, bump = gelu_parts(pre)
        hidden = (pre * cdf).astype(BF)
        hidden_all[at, :] = hidden
        slope = cdf + bump
        down = dot(hidden, w_down, NN)
        yield
        normal_2, inverse_2 = normalize(first + (down + vec(4)))
        mixed_out[at, :] = (normal_2 * vec(7) + vec(8)).astype(BF)
        cot = cot_ref[at, :]
        d_h2 = normalize_back(cot * vec(7), normal_2, inverse_2)
        d_down = d_h2.astype(BF)
        down_all[at, :] = d_down
        d_hidden = dot(d_down, w_down, NT)
        yield
        sums[7:8, :] += column_sum(cot * normal_2)
        sums[8:9, :] += column_sum(cot)
        d_pre = (d_hidden * slope).astype(BF)
        pre_all[at, :] = d_pre
        d_up = dot(d_pre, w_up, NT)
        yield
        d_first = d_h2 + d_up
        d_h1 = normalize_back(d_first * vec(5), normal_1, inverse_1)
        dh1_out[at, :] = d_h1
        d_branch = d_h1.astype(BF)
        branch_all[at, :] = d_branch
        datt_out[:, at] = dot(w_out, d_branch, NT).astype(BF)
        yield
        sums[5:6, :] += column_sum(d_first * normal_1)
        sums[6:7, :] += column_sum(d_first)

    tiles = [tile(number) for number in range(TILES)]
    while tiles:
        tiles = [one for one in tiles if next(one, True) is None]

    @pl.when(step == pl.num_programs(0) - 1)
    def _():
        ones = jnp.ones((16, TOK_DEV), BF)
        sums[2:3, :] = dot(ones, branch_all[...], NN)[:1]
        sums[3:4, :] = dot(ones, pre_all[...], NN)[:1]
        sums[4:5, :] = dot(ones, down_all[...], NN)[:1]
        vec_out[...] = sums[...]


def middle(place, tokens, cot, atts, vec, pieces, order):
    height = TILES * MT
    return pl.pallas_call(
        functools.partial(middle_kernel, order, len(pieces)),
        grid=(TOK_DEV // height,),
        in_specs=[SMEM] + [VM] * (5 + len(pieces)),
        out_specs=[VM] * 9,
        out_shape=[
            sds((TOK_DEV, D), BF),
            sds((TOK_DEV, D), F32),
            sds((D, TOK_DEV), BF),
            sds((16, D), F32),
        ]
        + [sds((TOK_DEV, D), BF)] * 5,
        scratch_shapes=[pltpu.VMEM((D, 3 * D), BF), pltpu.VMEM((16, D), F32)],
        compiler_params=params(MIDDLE_MIB),
        cost_estimate=cost(1e10, 1.2e7, 2**20),
        name="middle",
    )(place, tokens, cot, *atts, vec, *pieces)


def backward_kernel(n_shards, stages, plan, n_sets, n_inner, last, place, bias, tokens_t, vec_ref,
                    datt_ref, *refs):
    sets = [refs[6 * number : 6 * (number + 1)] for number in range(n_sets)]
    inner = refs[6 * n_sets : 6 * n_sets + n_inner]
    dw = refs[-1]
    n_g = 2 if stages else 1
    d_out, vec = refs[-3 - n_g : -1 - n_g]
    g_outs = refs[-1 - n_g : -1]
    vec[...] = vec_ref[...]
    halves = [slice(0, HALF), slice(HALF, TOK_DEV)]
    chains = [(place_out, *entry, mine) for place_out, entry in enumerate(plan) for mine in halves]

    def scores(chain):
        _, number, local, pair, mine = chain
        att_ref, lse_ref, krow_ref, vrow_ref, qt_ref, kt_ref = sets[number]
        here = slice(local * PAIR, (local + 1) * PAIR)
        q_t, d_t = qt_ref[here, mine], datt_ref[pair * PAIR : (pair + 1) * PAIR, mine]
        s = dot(krow_ref[local, mine, :], both_heads(q_t), NN)
        return q_t, d_t, s, dot(vrow_ref[local, mine, :], both_heads(d_t), NN)

    first = 0
    if inner:
        first = 3 * D
        first_all, hidden_all, branch_all, pre_all, down_all = inner
        attended = jnp.concatenate([sets[0][0][...], sets[1][0][...]], 0)
        products = [
            dot(attended, branch_all[...], NN),
            dot(first_all[...], pre_all[...], TN),
            dot(hidden_all[...], down_all[...], TN),
        ]
        for number, product in enumerate(products):
            dw[number % 2] = product
            cols = slice(number * D, (number + 1) * D)
            store_rows(g_outs, place, n_shards, stages, dw.at[number % 2], cols)
    ahead = scores(chains[0])
    for step, (place_out, number, local, pair, mine) in enumerate(chains):
        q_t, d_t, s, d_prob = ahead
        if step + 1 < len(chains):
            ahead = scores(chains[step + 1])
        att_ref, lse_ref, krow_ref, vrow_ref, qt_ref, kt_ref = sets[number]
        mask = bias[mine, :].astype(F32)
        lse = jnp.concatenate([lse_ref[local, 0:1, mine], lse_ref[local, 1:2, mine]], 1)
        here = slice(local * PAIR, (local + 1) * PAIR)
        product = d_t.astype(F32) * att_ref[here, mine].astype(F32)
        delta = jnp.concatenate([column_sum(product[:HEAD_DIM]), column_sum(product[HEAD_DIM:])], 1)
        prob = jnp.exp(s + jnp.concatenate([mask, mask], 1) - lse)
        d_s = (prob * (d_prob - delta)).astype(BF)
        prob_low = prob.astype(BF)
        for h in range(2):
            cols = slice(h * HALF, (h + 1) * HALF)
            head = slice(h * HEAD_DIM, (h + 1) * HEAD_DIM)
            k_t = kt_ref[local * PAIR + h * HEAD_DIM : local * PAIR + (h + 1) * HEAD_DIM, mine]
            d_q = dot(k_t, d_s[:, cols], NN) * (HEAD_DIM**-0.5)
            d_k = dot(q_t[head], d_s[:, cols], NT)
            d_v = dot(d_t[head], prob_low[:, cols], NT)
            for t, value in enumerate((d_q, d_k, d_v)):
                at = t * PAIR + h * HEAD_DIM
                d_out[place_out, at : at + HEAD_DIM, mine] = value.astype(BF)
        if mine.start == 0:
            continue
        trio = d_out[place_out]
        dw[place_out % 2, :, :TRIO] = dot(tokens_t[...], trio, NT)
        at = first + place_out * TRIO
        store_rows(
            g_outs, place, n_shards, stages, dw.at[place_out % 2, :, :TRIO], slice(at, at + TRIO)
        )
        total = dot(jnp.ones((16, TOK_DEV), BF), trio, NT)
        lanes = slice(pair * PAIR, (pair + 1) * PAIR)
        vec[0:1, lanes] = total[:1, :PAIR]
        vec[1:2, lanes] = total[:1, 2 * PAIR :]
    if stages and last:
        height = g_outs[0].shape[0]
        rows = D // n_shards
        for target, source, count in row_sources(place, n_shards, stages):
            at = pl.multiple_of(source // rows * rows, rows)
            g_outs[target // height][target % height : target % height + count, LATE:] = vec[
                :, pl.ds(at, rows)
            ].astype(BF)


def backward_attention(plan, last, place, mask, tokens_t, vec_sums, sets, d_t, inner, n_shards, stages, later):
    width = len(plan) * TRIO + (3 * D if inner else 0)
    if stages:
        shapes = [sds((D // 2, width + (PAIR if last else 0)), BF)] * 2
    else:
        shapes = [sds((D, width), BF)]
    flat = [value for saved in sets for value in saved]
    return pl.pallas_call(
        functools.partial(backward_kernel, n_shards, stages, plan, len(sets), len(inner), last),
        in_specs=[SMEM] + [VM] * (4 + len(flat) + len(inner)) + [ANY] * len(later),
        out_specs=[VM] * (2 + len(shapes)),
        out_shape=[sds((len(plan), TRIO, TOK_DEV), BF), sds((16, D), F32)] + shapes,
        scratch_shapes=[pltpu.VMEM((2, D, D), F32)],
        compiler_params=params(BACKWARD_MIB),
        cost_estimate=cost(5e9 * len(plan), 8e6, 2**21),
        name="backward_attention",
    )(place, mask, tokens_t, vec_sums, d_t, *flat, *inner, *later)


def input_grad_kernel(start, w_a, w_b, dh1_ref, trio_a, trio_b, *refs):
    out, turned = refs[-2:]
    trios = [ref.at[number] for ref in (trio_a, trio_b) for number in range(ref.shape[0])]
    for tile in range(TOK_DEV // QT):
        here = slice(tile * QT, (tile + 1) * QT)
        total = None
        for w_ref, parts in ((w_a, trios[:GROUP]), (w_b, trios[GROUP:])):
            term = dot(w_ref[...], jnp.concatenate([part[:, here] for part in parts], 0), NN)
            total = term if total is None else total + term
        turned[here, :] = dh1_ref[here, :] + total.T
    turn_rows(turned, (TOK_DEV - start[0]) & (TOK_DEV - 1), write_into(out))


def input_gradient(start, weights, d_h1, trios, later):
    return pl.pallas_call(
        input_grad_kernel,
        in_specs=[SMEM] + [VM] * 5 + [ANY] * len(later),
        out_specs=VM,
        out_shape=sds((TOK_DEV, D), F32),
        scratch_shapes=[pltpu.VMEM((TOK_DEV, D), F32)],
        compiler_params=params(),
        cost_estimate=cost(1, 1),
        name="input_gradient",
    )(start, *weights, d_h1, *trios, *later)


def adam(weight, grad, first, second, rate, decay):
    first = 0.5 * first + 0.5 * grad
    second = 0.5 * second + 0.5 * grad * grad
    fix = 1.0 - 0.5**STEP
    fixed = second * (1.0 / fix)
    update = first * (1.0 / fix) / (fixed * lax.rsqrt(fixed) + ADAM_EPS)
    return weight - rate * (update + decay * weight), first, second


def pair_parts(first, pairs):
    return [
        (slice(at, at + PAIR), 0, t * D + pair * PAIR)
        for number, pair in enumerate(pairs)
        for t in range(3)
        for at in [first + number * TRIO + t * PAIR]
    ]


EARLY_PARTS = [(slice(i * D, (i + 1) * D), i + 1, 0) for i in range(3)] + pair_parts(3 * D, range(FIRST))
LATE_PARTS = pair_parts(0, range(FIRST, PAIRS))


def adam_kernel(quick, limit, place, square_ref, *refs):
    n_grads = 4 if quick else 2
    grads = refs[:n_grads]
    vec_ref = refs[n_grads]
    states = refs[n_grads + 1 : n_grads + 16]
    outs = refs[n_grads + 16 : n_grads + 36]
    norm_out = refs[-1]
    step = pl.program_id(0)
    norm = jnp.sqrt(square_ref[0:1, 0:1])
    factor = limit / jnp.maximum(norm, limit)

    def write(number, where, target, grad, rate, decay):
        new, first, second = adam(
            states[number][where], grad * factor, states[5 + number][where],
            states[10 + number][where], rate, decay,
        )
        outs[number][target] = new
        outs[5 + number][target] = first
        outs[10 + number][target] = second
        outs[15 + number][target] = new.astype(BF)

    height = outs[0].shape[0]
    pieces = height // 16 if quick else 1
    rows = height // pieces
    for piece in range(pieces):
        here = pl.multiple_of(step * height + piece * rows, rows)
        if quick:
            mask = jnp.bitwise_xor(place[1], step * pieces + piece)
            at = pl.multiple_of(((mask >> 2) & 1) * 16 + ((mask >> 1) & 1) * 32, 16)
            odd = (mask & 1) == 1
        else:
            at = here
        for group, parts in enumerate((EARLY_PARTS, LATE_PARTS)):
            for cols, number, first in parts:
                if quick:
                    low, high = grads[2 * group], grads[2 * group + 1]
                    grad = jnp.where(odd, high[pl.ds(at, rows), cols], low[pl.ds(at, rows), cols])
                else:
                    grad = grads[group][pl.ds(at, rows), cols]
                there = slice(first, first + cols.stop - cols.start)
                write(
                    number, (pl.ds(here, rows), there), (slice(piece * rows, (piece + 1) * rows), there),
                    grad.astype(F32), 0.1, 0.01,
                )

    @pl.when(step == 0)
    def _():
        norm_out[0, 0] = norm[0, 0]
        vec_cols = states[4].shape[1]
        where = (slice(0, 9), slice(0, vec_cols))
        write(4, where, where, vec_ref[0:9, :vec_cols].astype(F32), 0.5, 0.0)


def adam_step(place, squares, limit, grads, vec_grad, weights, firsts, seconds, quick):
    steps = 4

    def spec(value):
        if value.shape[0] == 9:
            return whole(value.shape)
        return pl.BlockSpec((value.shape[0] // steps, value.shape[1]), lambda i: (i, 0))

    state = [spec(w) for w in weights]
    shapes = [sds(w.shape, F32) for w in weights]
    return pl.pallas_call(
        functools.partial(adam_kernel, quick, limit),
        grid=(steps,),
        in_specs=[SMEM] + [VM] * (17 + len(grads)),
        out_specs=state * 4 + [SMEM],
        out_shape=shapes * 3 + [sds(w.shape, BF) for w in weights] + [sds((1, 1), F32)],
        compiler_params=params(),
        name="adam",
    )(place, squares, *grads, vec_grad, *weights, *firsts, *seconds)


def swap(value, axis, mask):
    size = lax.axis_size(axis)
    return lax.ppermute(value, axis, [(i, i ^ mask) for i in range(size)])


def add_low(a, b):
    return (a.astype(F32) + b.astype(F32)).astype(BF)


def after(value, *others):
    return lax.optimization_barrier((value, others))[0]


def fold(keep, arrived):
    rows = keep.shape[0] // 2
    send = add_low(keep[rows:], arrived[rows:])
    return add_low(keep[:rows], arrived[:rows]), send


def squares_kernel(place, early, late, vec, out):
    total = []
    for piece in range(4):
        rows = slice(16 * piece, 16 * (piece + 1))
        first, second = early[rows, :].astype(F32), late[rows, :].astype(F32)
        total.append(jnp.sum(first * first) + jnp.sum(second * second))
    total = (total[0] + total[1]) + (total[2] + total[3])
    total = total + jnp.where((place[1] & 1) == 0, jnp.sum(vec[...] * vec[...]), 0.0)
    out[...] = jnp.full(out.shape, total, F32)


def half_squares(place, early, late, vec):
    return pl.pallas_call(
        squares_kernel,
        in_specs=[SMEM] + [VM] * 3,
        out_specs=VM,
        out_shape=sds((8, PAIR), F32),
        compiler_params=params(),
        cost_estimate=cost(1, 1),
        name="half_squares",
    )(place, early, late, vec)


def directly(value, axis, masks):
    return [swap(value, axis, mask) for mask in masks]


def four(value, others):
    return (value + others[0]) + (others[1] + others[2])


def join(held, arrived):
    return jnp.concatenate([held, arrived], 0)


def squares_of(value):
    value = value.astype(F32)
    return jnp.sum(value * value)


STAGES = (("narrow", 1), ("narrow", 2), ("wide", 1), ("wide", 2), ("wide", 4))


def body(
    tokens, cotangent, cells, present, generate,
    w_qkv, w_out, w_up, w_down, vectors,
    m_qkv, m_out, m_up, m_down, m_vec,
    v_qkv, v_out, v_up, v_down, v_vec,
):
    narrow, wide = lax.axis_size("narrow"), lax.axis_size("wide")
    quick = narrow == 4 and wide == 8
    stages = STAGES if quick else ()
    place = jnp.stack([lax.axis_index("narrow"), lax.axis_index("wide")]).astype(jnp.int32)
    shard = w_qkv.shape[0]

    low_a = pack_first(w_qkv, vectors)
    coded = jnp.where((present == 1) & (generate == 0), cells, cells + HIDDEN)
    tokens, tokens_t, cells, start = turn_tokens(tokens, after(coded, low_a))
    low_b, low_rest = pl.pallas_call(
        pack_second_kernel,
        in_specs=[VM] * 4 + [ANY],
        out_specs=[VM, VM],
        out_shape=[sds((shard, HW), BF), sds((shard, 3 * D), BF)],
        compiler_params=params(),
        name="pack_second",
    )(w_qkv, w_out, w_up, w_down, cells)
    if quick:
        y_a = after(swap(low_a, "narrow", 2), low_b)
        pieces_a = [low_a, swap(low_a, "narrow", 1), y_a, swap(y_a, "narrow", 1)]
        y_b = swap(after(low_b, y_a), "narrow", 2)
        c_b = swap(low_b, "narrow", 1)
        y_rest = swap(after(low_rest, y_a), "narrow", 2)
        c_rest = swap(low_rest, "narrow", 1)
        order = [(j, None, j) for j in range(4)]
        vec = jnp.zeros((8, PAIR), BF)
    else:
        pieces_a, pieces_b = [lax.all_gather(low_a, "narrow")], [lax.all_gather(low_b, "narrow")]
        pieces_rest = [lax.all_gather(low_rest, "narrow")]
        order = [(0, j, None) for j in range(narrow)]
        vec = lax.all_gather(vectors.astype(BF), "narrow", axis=1, tiled=True)
        vec = jnp.pad(vec, ((0, 7), (0, 0)))

    *saved_a, w_a, vec_full, tokens, mask = forward_attention(
        0, place, tokens, tokens_t, cells, vec, pieces_a, order
    )
    if quick:
        y_b, c_b = after(y_b, saved_a), after(c_b, saved_a)
        pieces_b = [low_b, c_b, y_b, swap(y_b, "narrow", 1)]
    *saved_b, w_b, vec_full, tokens = forward_attention(
        GROUP, place, tokens, tokens_t, mask, vec_full, pieces_b, order
    )
    if quick:
        y_rest, c_rest = after(y_rest, saved_b), after(c_rest, saved_b)
        d_rest = swap(y_rest, "narrow", 1)
        cotangent = turn_cotangent(start, cotangent, [y_rest])
        pieces_rest = [low_rest, c_rest, y_rest, after(d_rest, cotangent)]
    else:
        cotangent = turn_cotangent(start, cotangent, [])
    mixed, d_h1, d_t, vec_sums, *inner = middle(
        place, tokens, cotangent, (saved_a[0], saved_b[0]), vec_full, pieces_rest, order
    )
    sets = [saved_a, saved_b]
    plan = [(pair // GROUP, pair % GROUP, pair) for pair in range(PAIRS)]
    trio_a, vec_sums, *early = backward_attention(
        plan[:FIRST], False, place, mask, tokens_t, vec_sums, sets, d_t, inner, narrow, stages, []
    )
    later = []
    if quick:
        e_keep, e_send = early
        mixed = turn_back(start, mixed, [trio_a])
        e_keep, e_send = fold(e_keep, after(swap(e_send, "narrow", 1), mixed))
        e_arrived = swap(e_send, "narrow", 2)
        later = [e_send]
    trio_b, vec_sums, *late = backward_attention(
        plan[FIRST:], True, place, mask, tokens_t, vec_sums, sets, d_t, [], narrow, stages, later
    )
    weights, trios = (w_a, w_b), (trio_a, trio_b)

    if quick:
        b_keep, b_send = late
        b_arrived = swap(b_send, "narrow", 1)
        e_keep, e_send = fold(e_keep, after(e_arrived, trio_b))
        e_arrived = swap(e_send, "wide", 1)
        b_keep, b_send = fold(b_keep, after(b_arrived, e_send))
        b_arrived = swap(b_send, "narrow", 2)
        input_grad = input_gradient(start, weights, d_h1, trios, [b_send, e_send])
        e_keep, e_send = fold(e_keep, after(e_arrived, input_grad))
        e_arrived = swap(e_send, "wide", 2)
        b_keep, b_send = fold(b_keep, after(b_arrived, e_send))
        b_arrived = swap(b_send, "wide", 1)
        e_keep, e_send = fold(e_keep, after(e_arrived, b_send))
        e_arrived = swap(e_send, "wide", 4)
        b_keep, b_send = fold(b_keep, after(b_arrived, e_send))
        b_arrived = swap(b_send, "wide", 2)
        e_low = add_low(e_keep, after(e_arrived, b_send))
        e_arrived = swap(e_low, "wide", 4)
        b_keep, b_send = fold(b_keep, after(b_arrived, e_low))
        b_arrived = swap(b_send, "wide", 4)
        e_low = join(e_low, after(e_arrived, b_send))
        e_arrived = swap(e_low, "wide", 2)
        b_arrived = after(b_arrived, e_low)
        vec_total = b_keep[:, LATE:].astype(F32) + b_arrived[:, LATE:].astype(F32)
        b_low = add_low(b_keep[:, :LATE], b_arrived[:, :LATE])
        b_arrived = swap(b_low, "wide", 4)
        e_low = join(e_low, after(e_arrived, b_low))
        b_low = join(b_low, after(b_arrived, e_low))
        b_low = join(b_low, swap(b_low, "wide", 2))
        e_arrived, b_arrived = swap(e_low, "wide", 1), swap(b_low, "wide", 1)
        squares = half_squares(place, e_low, b_low, vec_total)
        squares = four(squares, directly(squares, "narrow", (1, 2, 3)))
        squares = squares + swap(squares, "wide", 1)
        grads = [e_low, after(e_arrived, squares), b_low, after(b_arrived, squares)]
    else:
        input_grad, mixed = input_gradient(start, weights, d_h1, trios, []), turn_back(start, mixed, [])
        vec_total = lax.psum_scatter(vec_sums, "narrow", scatter_dimension=1, tiled=True)
        vec_total = lax.psum(vec_total, "wide")
        grads = []
        for every in (early[0], late[0]):
            total = lax.psum_scatter(every, "narrow", scatter_dimension=0, tiled=True)
            grads.append(lax.psum(total.astype(F32), "wide"))
        squares = lax.psum(sum(squares_of(v) for v in grads + [vec_total]), "narrow")
        squares = jnp.full((8, PAIR), squares, F32)
    *updated, grad_norm = adam_step(
        place, squares, math.sqrt(TOK_DEV * wide * narrow), grads, vec_total,
        (w_qkv, w_out, w_up, w_down, vectors),
        (m_qkv, m_out, m_up, m_down, m_vec),
        (v_qkv, v_out, v_up, v_down, v_vec),
        quick,
    )
    return (mixed, input_grad, grad_norm[0, 0], *updated)


def solution(mesh):
    split = P(("wide", "narrow"), None)
    state = (P("narrow", None),) * 4 + (P(None, "narrow"),)
    return jax.shard_map(
        body,
        mesh=mesh,
        in_specs=(split,) * 5 + state * 3,
        out_specs=(split, split, P()) + state * 4,
        check_vma=False,
    )
```

profile of v0, /device:TPU:0, one launch (start us, length us, event | category | flops | bytes accessed | tf_op | source)
XLA Modules:
  0.0 113.1 jit_solution(4105745196110057331)
XLA Ops:
  0.7 1.9 %pack_first.1.refs_5_ = bf16[144,768]{1,0:T(8,128)(2,1)} custom-call(f32[128,1536]{1,0:T(8,128)} %refs_5_.1, f32[9,128]{1,0:T(8,128)} %refs_9_.1), custom_call_target="tpu_custom_call" | custom-call | tf_op jit(solution)/shard_map/pack_first/pallas_call | solution.py:104
  2.6 3.0 %collective-permute-start.1 = (bf16[144,768]{1,0:T(8,128)(2,1)}, bf16[144,768]{1,0:T(8,128)(2,1)S(1)}, u32[]{:S(2)}, u32[]{:S(2)}) collective-permute-start(bf16[144,768]{1,0:T(8,128)(2,1)} %pack_first.1.refs_5_), channel_id=1, source_target_pairs={{0,2},{1,3},{2,0},{3,1},{4,6},{5,7},{6,4},{7,5},{8,10},{9,11},{10,... | collective-permute-start | bytes 663560 | tf_op jit(solution)/shard_map/ppermute | solution.py:726
  11.3 1.7 %collective-permute-start.4 = (bf16[128,768]{1,0:T(8,128)(2,1)}, bf16[128,768]{1,0:T(8,128)(2,1)}, u32[]{:S(2)}, u32[]{:S(2)}) collective-permute-start(bf16[128,768]{1,0:T(8,128)(2,1)} %get-tuple-element.126.refs_5_), channel_id=1, source_target_pairs={{0,2},{1,3},{2,0},{3,1},{4,6},{5,7},{6,4},{7,5},{8,10},{9,11},{10,... | collective-permute-start | bytes 589832 | tf_op jit(solution)/shard_map/ppermute | solution.py:726
  14.6 6.0 %forward_attention.2 = (bf16[256,1024]{1,0:T(8,128)(2,1)S(1)}, f32[2,8,1024]{2,1,0:T(8,128)S(1)}, bf16[2,1024,128]{2,1,0:T(8,128)(2,1)S(1)}, bf16[2,1024,128]{2,...) custom-call(s32[2]{0:T(128)S(1)} %pad_add_fusion.refs_0_.place, ...), custom_call_target="tpu_custom_call" | custom-call | flops 1 | bytes 1 | tf_op jit(solution)/shard_map/forward_attention/pallas_call | solution.py:340
  22.5 5.8 %forward_attention.3 = (bf16[256,1024]{1,0:T(8,128)(2,1)S(1)}, f32[2,8,1024]{2,1,0:T(8,128)S(1)}, bf16[2,1024,128]{2,1,0:T(8,128)(2,1)S(1)}, bf16[2,1024,128]{2,...) custom-call(s32[2]{0:T(128)S(1)} %pad_add_fusion.refs_0_.place, ...), custom_call_target="tpu_custom_call" | custom-call | flops 1 | bytes 1 | tf_op jit(solution)/shard_map/forward_attention/pallas_call | solution.py:340
  30.1 9.8 %middle.1 = (bf16[1024,512]{1,0:T(8,128)(2,1)S(1)}, f32[1024,512]{1,0:T(8,128)S(1)}, bf16[512,1024]{1,0:T(8,128)(2,1)S(1)}, f32[16,512]{1,0:T(8,128)S(1)}, bf16[...) custom-call(s32[2]{0:T(128)S(1)} %pad_add_fusion.refs_0_.place, ...), custom_call_target="tpu_custom_call" | custom-call | flops 10000000000 | bytes 12000000 | tf_op jit(solution)/shard_map/middle/pallas_call | solution.py:484
  39.9 6.0 %backward_attention.2 = (bf16[1,384,1024]{2,1,0:T(8,128)(2,1)S(1)}, f32[16,512]{1,0:T(8,128)S(1)}, bf16[256,1920]{1,0:T(8,128)(2,1)S(1)}, bf16[256,1920]{1,0:T(8,128)(2,1)S(1)}) custom-call(s32[2]{0:T(128)S(1)} %pad_add_fusion.refs_0_.place, bf16[1024,512]{1,0:T(8,128)(2,1)S(1)} %get-tuple-element.117.refs_3_.bias, ...), custom_call_target="tpu_custom_call" | custom-call | flops 5000000000 | bytes 8000000 | tf_op jit(solution)/shard_map/backward_attention/pallas_call | solution.py:590
  46.4 2.3 %turn_back.1 = bf16[1024,512]{1,0:T(8,128)(2,1)} custom-call(s32[1]{0:T(128)} %get-tuple-element.110.start, bf16[1024,512]{1,0:T(8,128)(2,1)S(1)} %get-tuple-element.141.source, bf16[1,384,1024]{2,1,0:T(8,128)(2,1)S(1)} %get-tuple-element.149.refs_0_.trio_a), custom_call_target="tpu_custom_call" | custom-call | flops 1 | bytes 1 | tf_op jit(solution)/shard_map/turn_back/pallas_call | solution.py:230
  49.0 1.8 %collective-permute-start.11 = (bf16[128,1920]{1,0:T(8,128)(2,1)S(1)}, bf16[128,1920]{1,0:T(8,128)(2,1)S(1)}, u32[]{:S(2)}, u32[]{:S(2)}) collective-permute-start(bf16[128,1920]{1,0:T(8,128)(2,1)S(1)} %get-tuple-element.196.refs_12_), channel_id=1, source_target_pairs={{0,2},{1,3},{2,0},{3,1},{4,6},{5,7},{6,4},{7,5},{8,10},{9,11},{10,... | collective-permute-start | bytes 1474568 | tf_op jit(solution)/shard_map/ppermute | solution.py:726
  50.8 12.4 %backward_attention.3 = (bf16[3,384,1024]{2,1,0:T(8,128)(2,1)S(1)}, f32[16,512]{1,0:T(8,128)}, bf16[256,1280]{1,0:T(8,128)(2,1)S(1)}, bf16[256,1280]{1,0:T(8,128)(2,1)S(1)}) custom-call(s32[2]{0:T(128)S(1)} %pad_add_fusion.refs_0_.place, bf16[1024,512]{1,0:T(8,128)(2,1)S(1)} %get-tuple-element.117.refs_3_.bias, ...), custom_call_target="tpu_custom_call" | custom-call | flops 15000000512 | bytes 8000000 | tf_op jit(solution)/shard_map/backward_attention/pallas_call | solution.py:590
  66.0 4.4 %input_gradient.1 = f32[1024,512]{1,0:T(8,128)} custom-call(s32[1]{0:T(128)} %get-tuple-element.110.start, bf16[512,768]{1,0:T(8,128)(2,1)S(1)} %get-tuple-element.150.w_a, bf16[512,768]{1,0:T(8,128)(2,1)S(1)} %get-tuple-element.151.w_b, f32[1024,512]{1,0:T(8,128)S(1)} %get-tuple-element.152.dh1_ref, ...), custom_call_target="tpu_custom_call" | custom-call | flops 1 | bytes 1 | tf_op jit(solution)/shard_map/input_gradient/pallas_call | solution.py:616
  71.9 1.6 %collective-permute-start.13 = (bf16[32,1920]{1,0:T(8,128)(2,1)S(1)}, bf16[32,1920]{1,0:T(8,128)(2,1)S(1)}, u32[]{:S(2)}, u32[]{:S(2)}) collective-permute-start(bf16[32,1920]{1,0:T(8,128)(2,1)S(1)} %get-tuple-element.203), channel_id=1, source_target_pairs={{0,8},{4,12},{8,0},{12,4},{16,24},{20,28},{24,16},{28,20},{1,9},{5... | collective-permute-start | bytes 368648 | tf_op jit(solution)/shard_map/ppermute | solution.py:726
  73.6 1.7 %collective-permute-done.14 = bf16[128,1280]{1,0:T(8,128)(2,1)S(1)} collective-permute-done((bf16[128,1280]{1,0:T(8,128)(2,1)S(1)}, bf16[128,1280]{1,0:T(8,128)(2,1)S(1)}, u32[]{:S(2)}, u32[]{:S(2)}) %collective-permute-start.14) | collective-permute-done | bytes 327712 | tf_op jit(solution)/shard_map/ppermute | solution.py:726
  75.3 1.6 %collective-permute-start.16 = (bf16[64,1280]{1,0:T(8,128)(2,1)S(1)}, bf16[64,1280]{1,0:T(8,128)(2,1)S(1)}, u32[]{:S(2)}, u32[]{:S(2)}) collective-permute-start(bf16[64,1280]{1,0:T(8,128)(2,1)S(1)} %get-tuple-element.202), channel_id=1, source_target_pairs={{0,4},{4,0},{8,12},{12,8},{16,20},{20,16},{24,28},{28,24},{1,5},{5... | collective-permute-start | bytes 491528 | tf_op jit(solution)/shard_map/ppermute | solution.py:726
  77.0 2.7 %collective-permute-start.15 = (bf16[16,1920]{1,0:T(8,128)(2,1)S(1)}, bf16[16,1920]{1,0:T(8,128)(2,1)S(1)}, u32[]{:S(2)}, u32[]{:S(2)}) collective-permute-start(bf16[16,1920]{1,0:T(8,128)(2,1)S(1)} %add_convert_fusion.13), channel_id=1, source_target_pairs={{0,16},{4,20},{8,24},{12,28},{16,0},{20,4},{24,8},{28,12},{1,17},{... | collective-permute-start | bytes 184328 | tf_op jit(solution)/shard_map/ppermute | solution.py:726
  80.8 1.6 %collective-permute-start.18 = (bf16[32,1280]{1,0:T(8,128)(2,1)S(1)}, bf16[32,1280]{1,0:T(8,128)(2,1)S(1)}, u32[]{:S(2)}, u32[]{:S(2)}) collective-permute-start(bf16[32,1280]{1,0:T(8,128)(2,1)S(1)} %get-tuple-element.206), channel_id=1, source_target_pairs={{0,8},{4,12},{8,0},{12,4},{16,24},{20,28},{24,16},{28,20},{1,9},{5... | collective-permute-start | bytes 245768 | tf_op jit(solution)/shard_map/ppermute | solution.py:726
  82.5 2.7 %collective-permute-start.17 = (bf16[16,1920]{1,0:T(8,128)(2,1)S(1)}, bf16[16,1920]{1,0:T(8,128)(2,1)S(1)}, u32[]{:S(2)}, u32[]{:S(2)}) collective-permute-start(bf16[16,1920]{1,0:T(8,128)(2,1)S(1)} %add_convert_fusion.12), channel_id=1, source_target_pairs={{0,16},{4,20},{8,24},{12,28},{16,0},{20,4},{24,8},{28,12},{1,17},{... | collective-permute-start | bytes 184328 | tf_op jit(solution)/shard_map/ppermute | solution.py:726
  85.7 2.3 %collective-permute-start.20 = (bf16[16,1280]{1,0:T(8,128)(2,1)S(1)}, bf16[16,1280]{1,0:T(8,128)(2,1)S(1)}, u32[]{:S(2)}, u32[]{:S(2)}) collective-permute-start(bf16[16,1280]{1,0:T(8,128)(2,1)S(1)} %get-tuple-element.208), channel_id=1, source_target_pairs={{0,16},{4,20},{8,24},{12,28},{16,0},{20,4},{24,8},{28,12},{1,17},{... | collective-permute-start | bytes 122888 | tf_op jit(solution)/shard_map/ppermute | solution.py:726
  88.0 2.2 %collective-permute-start.19 = (bf16[32,1920]{1,0:T(8,128)(2,1)S(1)}, bf16[32,1920]{1,0:T(8,128)(2,1)S(1)}, u32[]{:S(2)}, u32[]{:S(2)}) collective-permute-start(bf16[32,1920]{1,0:T(8,128)(2,1)S(1)} %pad_maximum_fusion.2), channel_id=1, source_target_pairs={{0,8},{4,12},{8,0},{12,4},{16,24},{20,28},{24,16},{28,20},{1,9},{5... | collective-permute-start | bytes 368648 | tf_op jit(solution)/shard_map/ppermute | solution.py:726
  90.9 2.2 %collective-permute-start.21 = (bf16[16,1152]{1,0:T(8,128)(2,1)S(1)}, bf16[16,1152]{1,0:T(8,128)(2,1)S(1)}, u32[]{:S(2)}, u32[]{:S(2)}) collective-permute-start(bf16[16,1152]{1,0:T(8,128)(2,1)S(1)} %add_convert_fusion.17), channel_id=1, source_target_pairs={{0,16},{4,20},{8,24},{12,28},{16,0},{20,4},{24,8},{28,12},{1,17},{... | collective-permute-start | bytes 110600 | tf_op jit(solution)/shard_map/ppermute | solution.py:726
  93.2 2.7 %collective-permute-done.21 = bf16[16,1152]{1,0:T(8,128)(2,1)S(1)} collective-permute-done((bf16[16,1152]{1,0:T(8,128)(2,1)S(1)}, bf16[16,1152]{1,0:T(8,128)(2,1)S(1)}, u32[]{:S(2)}, u32[]{:S(2)}) %collective-permute-start.21) | collective-permute-done | bytes 36896 | tf_op jit(solution)/shard_map/ppermute | solution.py:726
  95.9 1.9 %collective-permute-start.22 = (bf16[32,1152]{1,0:T(8,128)(2,1)S(1)}, bf16[32,1152]{1,0:T(8,128)(2,1)S(1)}, u32[]{:S(2)}, u32[]{:S(2)}) collective-permute-start(bf16[32,1152]{1,0:T(8,128)(2,1)S(1)} %pad_maximum_fusion.3), channel_id=1, source_target_pairs={{0,8},{4,12},{8,0},{12,4},{16,24},{20,28},{24,16},{28,20},{1,9},{5... | collective-permute-start | bytes 221192 | tf_op jit(solution)/shard_map/ppermute | solution.py:726
  106.3 2.5 %collective-permute-done.26 = f32[8,128]{1,0:T(8,128)S(1)} collective-permute-done((f32[8,128]{1,0:T(8,128)S(1)}, f32[8,128]{1,0:T(8,128)S(1)}, u32[]{:S(2)}, u32[]{:S(2)}) %collective-permute-start.26) | collective-permute-done | bytes 4128 | tf_op jit(solution)/shard_map/ppermute | solution.py:726
  108.9 4.0 %adam.1 = (f32[128,1536]{1,0:T(8,128)}, f32[128,512]{1,0:T(8,128)}, f32[128,512]{1,0:T(8,128)}, f32[128,512]{1,0:T(8,128)}, f32[9,128]{1,0:T(8,128)}, /*index=5*...) custom-call(s32[2]{0:T(128)S(1)} %pad_add_fusion.refs_0_.place, ...), custom_call_target="tpu_custom_call" | custom-call | tf_op jit(solution)/shard_map/adam/pallas_call | solution.py:713
  (107 shorter events, 27.0 us)
Async XLA Ops:
  2.6 8.7 %collective-permute-start.1 = (bf16[144,768]{1,0:T(8,128)(2,1)}, bf16[144,768]{1,0:T(8,128)(2,1)S(1)}, u32[]{:S(2)}, u32[]{:S(2)}) collective-permute-start(bf16[144,768]{1,0:T(8,128)(2,1)} %pack_first.1.refs_5_), channel_id=1, source_target_pairs={{0,2},{1,3},{2,0},{3,1},{4,6},{5,7},{6,4},{7,5},{8,10},{9,11},{10,... | collective-permute-start | bytes 663560 | tf_op jit(solution)/shard_map/ppermute | solution.py:726
  5.6 7.7 %collective-permute-start = (bf16[144,768]{1,0:T(8,128)(2,1)}, bf16[144,768]{1,0:T(8,128)(2,1)}, u32[]{:S(2)}, u32[]{:S(2)}) collective-permute-start(bf16[144,768]{1,0:T(8,128)(2,1)} %pack_first.1.refs_5_), channel_id=1, source_target_pairs={{0,1},{1,0},{2,3},{3,2},{4,5},{5,4},{6,7},{7,6},{8,9},{9,8},{10,11... | collective-permute-start | bytes 663560 | tf_op jit(solution)/shard_map/ppermute | solution.py:726
  11.3 9.4 %collective-permute-start.4 = (bf16[128,768]{1,0:T(8,128)(2,1)}, bf16[128,768]{1,0:T(8,128)(2,1)}, u32[]{:S(2)}, u32[]{:S(2)}) collective-permute-start(bf16[128,768]{1,0:T(8,128)(2,1)} %get-tuple-element.126.refs_5_), channel_id=1, source_target_pairs={{0,2},{1,3},{2,0},{3,1},{4,6},{5,7},{6,4},{7,5},{8,10},{9,11},{10,... | collective-permute-start | bytes 589832 | tf_op jit(solution)/shard_map/ppermute | solution.py:726
  13.0 15.3 %collective-permute-start.6 = (bf16[128,1536]{1,0:T(8,128)(2,1)}, bf16[128,1536]{1,0:T(8,128)(2,1)S(1)}, u32[]{:S(2)}, u32[]{:S(2)}) collective-permute-start(bf16[128,1536]{1,0:T(8,128)(2,1)} %get-tuple-element.130.refs_6_), channel_id=1, source_target_pairs={{0,2},{1,3},{2,0},{3,1},{4,6},{5,7},{6,4},{7,5},{8,10},{9,11},{10,... | collective-permute-start | bytes 1179656 | tf_op jit(solution)/shard_map/ppermute | solution.py:726
  13.3 8.0 %collective-permute-start.3 = (bf16[128,768]{1,0:T(8,128)(2,1)}, bf16[128,768]{1,0:T(8,128)(2,1)}, u32[]{:S(2)}, u32[]{:S(2)}) collective-permute-start(bf16[128,768]{1,0:T(8,128)(2,1)} %get-tuple-element.126.refs_5_), channel_id=1, source_target_pairs={{0,1},{1,0},{2,3},{3,2},{4,5},{5,4},{6,7},{7,6},{8,9},{9,8},{10,11... | collective-permute-start | bytes 589832 | tf_op jit(solution)/shard_map/ppermute | solution.py:726
  21.2 7.6 %collective-permute-start.7 = (bf16[128,1536]{1,0:T(8,128)(2,1)}, bf16[128,1536]{1,0:T(8,128)(2,1)S(1)}, u32[]{:S(2)}, u32[]{:S(2)}) collective-permute-start(bf16[128,1536]{1,0:T(8,128)(2,1)} %get-tuple-element.130.refs_6_), channel_id=1, source_target_pairs={{0,1},{1,0},{2,3},{3,2},{4,5},{5,4},{6,7},{7,6},{8,9},{9,8},{10,11... | collective-permute-start | bytes 1179656 | tf_op jit(solution)/shard_map/ppermute | solution.py:726
  49.0 14.2 %collective-permute-start.11 = (bf16[128,1920]{1,0:T(8,128)(2,1)S(1)}, bf16[128,1920]{1,0:T(8,128)(2,1)S(1)}, u32[]{:S(2)}, u32[]{:S(2)}) collective-permute-start(bf16[128,1920]{1,0:T(8,128)(2,1)S(1)} %get-tuple-element.196.refs_12_), channel_id=1, source_target_pairs={{0,2},{1,3},{2,0},{3,1},{4,6},{5,7},{6,4},{7,5},{8,10},{9,11},{10,... | collective-permute-start | bytes 1474568 | tf_op jit(solution)/shard_map/ppermute | solution.py:726
  63.3 8.4 %collective-permute-start.12 = (bf16[64,1920]{1,0:T(8,128)(2,1)S(1)}, bf16[64,1920]{1,0:T(8,128)(2,1)S(1)}, u32[]{:S(2)}, u32[]{:S(2)}) collective-permute-start(bf16[64,1920]{1,0:T(8,128)(2,1)S(1)} %get-tuple-element.200.refs_1_), channel_id=1, source_target_pairs={{0,4},{4,0},{8,12},{12,8},{16,20},{20,16},{24,28},{28,24},{1,5},{5... | collective-permute-start | bytes 737288 | tf_op jit(solution)/shard_map/ppermute | solution.py:726
  65.4 9.8 %collective-permute-start.14 = (bf16[128,1280]{1,0:T(8,128)(2,1)S(1)}, bf16[128,1280]{1,0:T(8,128)(2,1)S(1)}, u32[]{:S(2)}, u32[]{:S(2)}) collective-permute-start(bf16[128,1280]{1,0:T(8,128)(2,1)S(1)} %get-tuple-element.198.refs_0_), channel_id=1, source_target_pairs={{0,2},{1,3},{2,0},{3,1},{4,6},{5,7},{6,4},{7,5},{8,10},{9,11},{10,... | collective-permute-start | bytes 983048 | tf_op jit(solution)/shard_map/ppermute | solution.py:726
  71.9 5.0 %collective-permute-start.13 = (bf16[32,1920]{1,0:T(8,128)(2,1)S(1)}, bf16[32,1920]{1,0:T(8,128)(2,1)S(1)}, u32[]{:S(2)}, u32[]{:S(2)}) collective-permute-start(bf16[32,1920]{1,0:T(8,128)(2,1)S(1)} %get-tuple-element.203), channel_id=1, source_target_pairs={{0,8},{4,12},{8,0},{12,4},{16,24},{20,28},{24,16},{28,20},{1,9},{5... | collective-permute-start | bytes 368648 | tf_op jit(solution)/shard_map/ppermute | solution.py:726
  75.3 5.5 %collective-permute-start.16 = (bf16[64,1280]{1,0:T(8,128)(2,1)S(1)}, bf16[64,1280]{1,0:T(8,128)(2,1)S(1)}, u32[]{:S(2)}, u32[]{:S(2)}) collective-permute-start(bf16[64,1280]{1,0:T(8,128)(2,1)S(1)} %get-tuple-element.202), channel_id=1, source_target_pairs={{0,4},{4,0},{8,12},{12,8},{16,20},{20,16},{24,28},{28,24},{1,5},{5... | collective-permute-start | bytes 491528 | tf_op jit(solution)/shard_map/ppermute | solution.py:726
  77.0 5.5 %collective-permute-start.15 = (bf16[16,1920]{1,0:T(8,128)(2,1)S(1)}, bf16[16,1920]{1,0:T(8,128)(2,1)S(1)}, u32[]{:S(2)}, u32[]{:S(2)}) collective-permute-start(bf16[16,1920]{1,0:T(8,128)(2,1)S(1)} %add_convert_fusion.13), channel_id=1, source_target_pairs={{0,16},{4,20},{8,24},{12,28},{16,0},{20,4},{24,8},{28,12},{1,17},{... | collective-permute-start | bytes 184328 | tf_op jit(solution)/shard_map/ppermute | solution.py:726
  80.8 4.9 %collective-permute-start.18 = (bf16[32,1280]{1,0:T(8,128)(2,1)S(1)}, bf16[32,1280]{1,0:T(8,128)(2,1)S(1)}, u32[]{:S(2)}, u32[]{:S(2)}) collective-permute-start(bf16[32,1280]{1,0:T(8,128)(2,1)S(1)} %get-tuple-element.206), channel_id=1, source_target_pairs={{0,8},{4,12},{8,0},{12,4},{16,24},{20,28},{24,16},{28,20},{1,9},{5... | collective-permute-start | bytes 245768 | tf_op jit(solution)/shard_map/ppermute | solution.py:726
  82.5 5.5 %collective-permute-start.17 = (bf16[16,1920]{1,0:T(8,128)(2,1)S(1)}, bf16[16,1920]{1,0:T(8,128)(2,1)S(1)}, u32[]{:S(2)}, u32[]{:S(2)}) collective-permute-start(bf16[16,1920]{1,0:T(8,128)(2,1)S(1)} %add_convert_fusion.12), channel_id=1, source_target_pairs={{0,16},{4,20},{8,24},{12,28},{16,0},{20,4},{24,8},{28,12},{1,17},{... | collective-permute-start | bytes 184328 | tf_op jit(solution)/shard_map/ppermute | solution.py:726
  85.7 5.2 %collective-permute-start.20 = (bf16[16,1280]{1,0:T(8,128)(2,1)S(1)}, bf16[16,1280]{1,0:T(8,128)(2,1)S(1)}, u32[]{:S(2)}, u32[]{:S(2)}) collective-permute-start(bf16[16,1280]{1,0:T(8,128)(2,1)S(1)} %get-tuple-element.208), channel_id=1, source_target_pairs={{0,16},{4,20},{8,24},{12,28},{16,0},{20,4},{24,8},{28,12},{1,17},{... | collective-permute-start | bytes 122888 | tf_op jit(solution)/shard_map/ppermute | solution.py:726
  88.0 5.1 %collective-permute-start.19 = (bf16[32,1920]{1,0:T(8,128)(2,1)S(1)}, bf16[32,1920]{1,0:T(8,128)(2,1)S(1)}, u32[]{:S(2)}, u32[]{:S(2)}) collective-permute-start(bf16[32,1920]{1,0:T(8,128)(2,1)S(1)} %pad_maximum_fusion.2), channel_id=1, source_target_pairs={{0,8},{4,12},{8,0},{12,4},{16,24},{20,28},{24,16},{28,20},{1,9},{5... | collective-permute-start | bytes 368648 | tf_op jit(solution)/shard_map/ppermute | solution.py:726
  90.9 4.9 %collective-permute-start.21 = (bf16[16,1152]{1,0:T(8,128)(2,1)S(1)}, bf16[16,1152]{1,0:T(8,128)(2,1)S(1)}, u32[]{:S(2)}, u32[]{:S(2)}) collective-permute-start(bf16[16,1152]{1,0:T(8,128)(2,1)S(1)} %add_convert_fusion.17), channel_id=1, source_target_pairs={{0,16},{4,20},{8,24},{12,28},{16,0},{20,4},{24,8},{28,12},{1,17},{... | collective-permute-start | bytes 110600 | tf_op jit(solution)/shard_map/ppermute | solution.py:726
  95.9 4.4 %collective-permute-start.22 = (bf16[32,1152]{1,0:T(8,128)(2,1)S(1)}, bf16[32,1152]{1,0:T(8,128)(2,1)S(1)}, u32[]{:S(2)}, u32[]{:S(2)}) collective-permute-start(bf16[32,1152]{1,0:T(8,128)(2,1)S(1)} %pad_maximum_fusion.3), channel_id=1, source_target_pairs={{0,8},{4,12},{8,0},{12,4},{16,24},{20,28},{24,16},{28,20},{1,9},{5... | collective-permute-start | bytes 221192 | tf_op jit(solution)/shard_map/ppermute | solution.py:726
  97.7 11.0 %collective-permute-start.27 = (bf16[64,1920]{1,0:T(8,128)(2,1)S(1)}, bf16[64,1920]{1,0:T(8,128)(2,1)S(1)}, u32[]{:S(2)}, u32[]{:S(2)}) collective-permute-start(bf16[64,1920]{1,0:T(8,128)(2,1)S(1)} %pad_maximum_fusion.early.refs_0_), channel_id=1, source_target_pairs={{0,4},{4,0},{8,12},{12,8},{16,20},{20,16},{24,28},{28,24},{1,5},{5... | collective-permute-start | bytes 737288 | tf_op jit(solution)/shard_map/ppermute | solution.py:726
  101.0 3.4 %collective-permute-start.25 = (f32[8,128]{1,0:T(8,128)S(1)}, f32[8,128]{1,0:T(8,128)S(1)}, u32[]{:S(2)}, u32[]{:S(2)}) collective-permute-start(f32[8,128]{1,0:T(8,128)S(1)} %half_squares.1), channel_id=1, source_target_pairs={{0,3},{1,2},{2,1},{3,0},{4,7},{5,6},{6,5},{7,4},{8,11},{9,10},{10,... | collective-permute-start | bytes 12296 | tf_op jit(solution)/shard_map/ppermute | solution.py:726
  101.1 3.7 %collective-permute-start.24 = (f32[8,128]{1,0:T(8,128)S(1)}, f32[8,128]{1,0:T(8,128)S(1)}, u32[]{:S(2)}, u32[]{:S(2)}) collective-permute-start(f32[8,128]{1,0:T(8,128)S(1)} %half_squares.1), channel_id=1, source_target_pairs={{0,2},{1,3},{2,0},{3,1},{4,6},{5,7},{6,4},{7,5},{8,10},{9,11},{10,... | collective-permute-start | bytes 12296 | tf_op jit(solution)/shard_map/ppermute | solution.py:726
  101.4 3.3 %collective-permute-start.23 = (f32[8,128]{1,0:T(8,128)S(1)}, f32[8,128]{1,0:T(8,128)S(1)}, u32[]{:S(2)}, u32[]{:S(2)}) collective-permute-start(f32[8,128]{1,0:T(8,128)S(1)} %half_squares.1), channel_id=1, source_target_pairs={{0,1},{1,0},{2,3},{3,2},{4,5},{5,4},{6,7},{7,6},{8,9},{9,8},{10,11... | collective-permute-start | bytes 12296 | tf_op jit(solution)/shard_map/ppermute | solution.py:726
  102.9 5.9 %collective-permute-start.28 = (bf16[64,1152]{1,0:T(8,128)(2,1)S(1)}, bf16[64,1152]{1,0:T(8,128)(2,1)S(1)}, u32[]{:S(2)}, u32[]{:S(2)}) collective-permute-start(bf16[64,1152]{1,0:T(8,128)(2,1)S(1)} %pad_maximum_fusion.1.late.refs_2_), channel_id=1, source_target_pairs={{0,4},{4,0},{8,12},{12,8},{16,20},{20,16},{24,28},{28,24},{1,5},{5... | collective-permute-start | bytes 442376 | tf_op jit(solution)/shard_map/ppermute | solution.py:726
  104.8 4.0 %collective-permute-start.26 = (f32[8,128]{1,0:T(8,128)S(1)}, f32[8,128]{1,0:T(8,128)S(1)}, u32[]{:S(2)}, u32[]{:S(2)}) collective-permute-start(f32[8,128]{1,0:T(8,128)S(1)} %add_add_fusion), channel_id=1, source_target_pairs={{0,4},{4,0},{8,12},{12,8},{16,20},{20,16},{24,28},{28,24},{1,5},{5... | collective-permute-start | bytes 12296 | tf_op jit(solution)/shard_map/ppermute | solution.py:726
  (25 other events, 471.3 us)
where the time goes:
time: 113 us
  Pallas kernels  56.5 us (50%)
  starting transfers between devices  35.8 us (32%)
  waiting for transfers between devices  14.3 us (13%)
  local copies, waits for them, and re-layouts  3.5 us (3%)
  other arithmetic  1.67 us (1%)
  between operations  1.25 us (1%)
    ppermute x29, starting transfers between devices, swap(): return lax.ppermute(value, axis, [(i, i ^ mask) for i in range(size)])  35.8 us
    pallas_call x2, Pallas kernels, backward_attention(): pl.pallas_call(functools.partial(backward_kernel, n_shards, stages, plan,...  18.4 us
    ppermute x29, waiting for transfers between devices, swap(): return lax.ppermute(value, axis, [(i, i ^ mask) for i in range(size)])  14.3 us
    pallas_call x2, Pallas kernels, forward_attention(): pl.pallas_call(functools.partial(forward_kernel, order, len(pieces), base...  11.8 us
    pallas_call x1, Pallas kernels, middle(): pl.pallas_call(functools.partial(middle_kernel, order, len(pieces)), grid...  9.79 us
    pallas_call x1, Pallas kernels, input_gradient(): pl.pallas_call(input_grad_kernel, in_specs=[SMEM] + [VM] * 5 + [ANY] * le...  4.4 us
    pallas_call x1, Pallas kernels, adam_step(): pl.pallas_call(functools.partial(adam_kernel, quick, limit), grid=(steps,...  3.98 us
    unnamed x40, local copies, waits for them, and re-layouts  3.5 us
  transfers between devices with their start and end apart: 29, of which 14 were waited for; matrix products, arithmetic and copies ran while one was open for 1% of the time, Pallas kernels for 31%

commit v1 on v0

--- a/solution.py
+++ b/solution.py
@@ -701,7 +701,7 @@
 
 
 def adam_step(place, squares, limit, grads, vec_grad, weights, firsts, seconds, quick):
-    steps = 4
+    steps = 2
 
     def spec(value):
         if value.shape[0] == 9:

time: 113 us -> 113 us (level)
  no operation moved by 1% of the time
where the time goes in v1:
time: 113 us
  Pallas kernels  56.6 us (50%)
  starting transfers between devices  35.8 us (32%)
  waiting for transfers between devices  14.1 us (12%)
  local copies, waits for them, and re-layouts  3.5 us (3%)
  other arithmetic  1.67 us (1%)
  between operations  1.27 us (1%)
    ppermute x29, starting transfers between devices, swap(): return lax.ppermute(value, axis, [(i, i ^ mask) for i in range(size)])  35.8 us
    pallas_call x2, Pallas kernels, backward_attention(): pl.pallas_call(functools.partial(backward_kernel, n_shards, stages, plan,...  18.4 us
    ppermute x29, waiting for transfers between devices, swap(): return lax.ppermute(value, axis, [(i, i ^ mask) for i in range(size)])  14.1 us
    pallas_call x2, Pallas kernels, forward_attention(): pl.pallas_call(functools.partial(forward_kernel, order, len(pieces), base...  11.8 us
    pallas_call x1, Pallas kernels, middle(): pl.pallas_call(functools.partial(middle_kernel, order, len(pieces)), grid...  9.79 us
    pallas_call x1, Pallas kernels, input_gradient(): pl.pallas_call(input_grad_kernel, in_specs=[SMEM] + [VM] * 5 + [ANY] * le...  4.66 us
    pallas_call x1, Pallas kernels, adam_step(): pl.pallas_call(functools.partial(adam_kernel, quick, limit), grid=(steps,...  3.79 us
    unnamed x40, local copies, waits for them, and re-layouts  3.5 us
  transfers between devices with their start and end apart: 29, of which 14 were waited for; matrix products, arithmetic and copies ran while one was open for 1% of the time, Pallas kernels for 31%

profile of v1, /device:TPU:0, one launch (start us, length us, event | category | flops | bytes accessed | tf_op | source)
XLA Modules:
  0.0 112.9 jit_solution(7159187237929854349)
XLA Ops:
  0.7 1.9 %pack_first.1.refs_5_ = bf16[144,768]{1,0:T(8,128)(2,1)} custom-call(f32[128,1536]{1,0:T(8,128)} %refs_5_.1, f32[9,128]{1,0:T(8,128)} %refs_9_.1), custom_call_target="tpu_custom_call" | custom-call | tf_op jit(solution)/shard_map/pack_first/pallas_call | solution.py:104
  2.6 3.0 %collective-permute-start.1 = (bf16[144,768]{1,0:T(8,128)(2,1)}, bf16[144,768]{1,0:T(8,128)(2,1)S(1)}, u32[]{:S(2)}, u32[]{:S(2)}) collective-permute-start(bf16[144,768]{1,0:T(8,128)(2,1)} %pack_first.1.refs_5_), channel_id=1, source_target_pairs={{0,2},{1,3},{2,0},{3,1},{4,6},{5,7},{6,4},{7,5},{8,10},{9,11},{10,... | collective-permute-start | bytes 663560 | tf_op jit(solution)/shard_map/ppermute | solution.py:726
  11.3 1.7 %collective-permute-start.4 = (bf16[128,768]{1,0:T(8,128)(2,1)}, bf16[128,768]{1,0:T(8,128)(2,1)}, u32[]{:S(2)}, u32[]{:S(2)}) collective-permute-start(bf16[128,768]{1,0:T(8,128)(2,1)} %get-tuple-element.126.refs_5_), channel_id=1, source_target_pairs={{0,2},{1,3},{2,0},{3,1},{4,6},{5,7},{6,4},{7,5},{8,10},{9,11},{10,... | collective-permute-start | bytes 589832 | tf_op jit(solution)/shard_map/ppermute | solution.py:726
  14.6 6.0 %forward_attention.2 = (bf16[256,1024]{1,0:T(8,128)(2,1)S(1)}, f32[2,8,1024]{2,1,0:T(8,128)S(1)}, bf16[2,1024,128]{2,1,0:T(8,128)(2,1)S(1)}, bf16[2,1024,128]{2,...) custom-call(s32[2]{0:T(128)S(1)} %pad_add_fusion.refs_0_.place, ...), custom_call_target="tpu_custom_call" | custom-call | flops 1 | bytes 1 | tf_op jit(solution)/shard_map/forward_attention/pallas_call | solution.py:340
  22.5 5.8 %forward_attention.3 = (bf16[256,1024]{1,0:T(8,128)(2,1)S(1)}, f32[2,8,1024]{2,1,0:T(8,128)S(1)}, bf16[2,1024,128]{2,1,0:T(8,128)(2,1)S(1)}, bf16[2,1024,128]{2,...) custom-call(s32[2]{0:T(128)S(1)} %pad_add_fusion.refs_0_.place, ...), custom_call_target="tpu_custom_call" | custom-call | flops 1 | bytes 1 | tf_op jit(solution)/shard_map/forward_attention/pallas_call | solution.py:340
  30.1 9.8 %middle.1 = (bf16[1024,512]{1,0:T(8,128)(2,1)S(1)}, f32[1024,512]{1,0:T(8,128)S(1)}, bf16[512,1024]{1,0:T(8,128)(2,1)S(1)}, f32[16,512]{1,0:T(8,128)S(1)}, bf16[...) custom-call(s32[2]{0:T(128)S(1)} %pad_add_fusion.refs_0_.place, ...), custom_call_target="tpu_custom_call" | custom-call | flops 10000000000 | bytes 12000000 | tf_op jit(solution)/shard_map/middle/pallas_call | solution.py:484
  39.9 6.0 %backward_attention.2 = (bf16[1,384,1024]{2,1,0:T(8,128)(2,1)S(1)}, f32[16,512]{1,0:T(8,128)S(1)}, bf16[256,1920]{1,0:T(8,128)(2,1)S(1)}, bf16[256,1920]{1,0:T(8,128)(2,1)S(1)}) custom-call(s32[2]{0:T(128)S(1)} %pad_add_fusion.refs_0_.place, bf16[1024,512]{1,0:T(8,128)(2,1)S(1)} %get-tuple-element.117.refs_3_.bias, ...), custom_call_target="tpu_custom_call" | custom-call | flops 5000000000 | bytes 8000000 | tf_op jit(solution)/shard_map/backward_attention/pallas_call | solution.py:590
  46.4 2.3 %turn_back.1 = bf16[1024,512]{1,0:T(8,128)(2,1)} custom-call(s32[1]{0:T(128)} %get-tuple-element.110.start, bf16[1024,512]{1,0:T(8,128)(2,1)S(1)} %get-tuple-element.141.source, bf16[1,384,1024]{2,1,0:T(8,128)(2,1)S(1)} %get-tuple-element.149.refs_0_.trio_a), custom_call_target="tpu_custom_call" | custom-call | flops 1 | bytes 1 | tf_op jit(solution)/shard_map/turn_back/pallas_call | solution.py:230
  49.0 1.8 %collective-permute-start.11 = (bf16[128,1920]{1,0:T(8,128)(2,1)S(1)}, bf16[128,1920]{1,0:T(8,128)(2,1)S(1)}, u32[]{:S(2)}, u32[]{:S(2)}) collective-permute-start(bf16[128,1920]{1,0:T(8,128)(2,1)S(1)} %get-tuple-element.196.refs_12_), channel_id=1, source_target_pairs={{0,2},{1,3},{2,0},{3,1},{4,6},{5,7},{6,4},{7,5},{8,10},{9,11},{10,... | collective-permute-start | bytes 1474568 | tf_op jit(solution)/shard_map/ppermute | solution.py:726
  50.8 12.4 %backward_attention.3 = (bf16[3,384,1024]{2,1,0:T(8,128)(2,1)S(1)}, f32[16,512]{1,0:T(8,128)}, bf16[256,1280]{1,0:T(8,128)(2,1)S(1)}, bf16[256,1280]{1,0:T(8,128)(2,1)S(1)}) custom-call(s32[2]{0:T(128)S(1)} %pad_add_fusion.refs_0_.place, bf16[1024,512]{1,0:T(8,128)(2,1)S(1)} %get-tuple-element.117.refs_3_.bias, ...), custom_call_target="tpu_custom_call" | custom-call | flops 15000000512 | bytes 8000000 | tf_op jit(solution)/shard_map/backward_attention/pallas_call | solution.py:590
  66.0 4.7 %input_gradient.1 = f32[1024,512]{1,0:T(8,128)} custom-call(s32[1]{0:T(128)} %get-tuple-element.110.start, bf16[512,768]{1,0:T(8,128)(2,1)S(1)} %get-tuple-element.150.w_a, bf16[512,768]{1,0:T(8,128)(2,1)S(1)} %get-tuple-element.151.w_b, f32[1024,512]{1,0:T(8,128)S(1)} %get-tuple-element.152.dh1_ref, ...), custom_call_target="tpu_custom_call" | custom-call | flops 1 | bytes 1 | tf_op jit(solution)/shard_map/input_gradient/pallas_call | solution.py:616
  71.9 1.6 %collective-permute-start.13 = (bf16[32,1920]{1,0:T(8,128)(2,1)S(1)}, bf16[32,1920]{1,0:T(8,128)(2,1)S(1)}, u32[]{:S(2)}, u32[]{:S(2)}) collective-permute-start(bf16[32,1920]{1,0:T(8,128)(2,1)S(1)} %get-tuple-element.203), channel_id=1, source_target_pairs={{0,8},{4,12},{8,0},{12,4},{16,24},{20,28},{24,16},{28,20},{1,9},{5... | collective-permute-start | bytes 368648 | tf_op jit(solution)/shard_map/ppermute | solution.py:726
  73.6 1.7 %collective-permute-done.14 = bf16[128,1280]{1,0:T(8,128)(2,1)S(1)} collective-permute-done((bf16[128,1280]{1,0:T(8,128)(2,1)S(1)}, bf16[128,1280]{1,0:T(8,128)(2,1)S(1)}, u32[]{:S(2)}, u32[]{:S(2)}) %collective-permute-start.14) | collective-permute-done | bytes 327712 | tf_op jit(solution)/shard_map/ppermute | solution.py:726
  75.3 1.6 %collective-permute-start.16 = (bf16[64,1280]{1,0:T(8,128)(2,1)S(1)}, bf16[64,1280]{1,0:T(8,128)(2,1)S(1)}, u32[]{:S(2)}, u32[]{:S(2)}) collective-permute-start(bf16[64,1280]{1,0:T(8,128)(2,1)S(1)} %get-tuple-element.202), channel_id=1, source_target_pairs={{0,4},{4,0},{8,12},{12,8},{16,20},{20,16},{24,28},{28,24},{1,5},{5... | collective-permute-start | bytes 491528 | tf_op jit(solution)/shard_map/ppermute | solution.py:726
  77.0 2.7 %collective-permute-start.15 = (bf16[16,1920]{1,0:T(8,128)(2,1)S(1)}, bf16[16,1920]{1,0:T(8,128)(2,1)S(1)}, u32[]{:S(2)}, u32[]{:S(2)}) collective-permute-start(bf16[16,1920]{1,0:T(8,128)(2,1)S(1)} %add_convert_fusion.13), channel_id=1, source_target_pairs={{0,16},{4,20},{8,24},{12,28},{16,0},{20,4},{24,8},{28,12},{1,17},{... | collective-permute-start | bytes 184328 | tf_op jit(solution)/shard_map/ppermute | solution.py:726
  80.8 1.6 %collective-permute-start.18 = (bf16[32,1280]{1,0:T(8,128)(2,1)S(1)}, bf16[32,1280]{1,0:T(8,128)(2,1)S(1)}, u32[]{:S(2)}, u32[]{:S(2)}) collective-permute-start(bf16[32,1280]{1,0:T(8,128)(2,1)S(1)} %get-tuple-element.206), channel_id=1, source_target_pairs={{0,8},{4,12},{8,0},{12,4},{16,24},{20,28},{24,16},{28,20},{1,9},{5... | collective-permute-start | bytes 245768 | tf_op jit(solution)/shard_map/ppermute | solution.py:726
  82.5 2.7 %collective-permute-start.17 = (bf16[16,1920]{1,0:T(8,128)(2,1)S(1)}, bf16[16,1920]{1,0:T(8,128)(2,1)S(1)}, u32[]{:S(2)}, u32[]{:S(2)}) collective-permute-start(bf16[16,1920]{1,0:T(8,128)(2,1)S(1)} %add_convert_fusion.12), channel_id=1, source_target_pairs={{0,16},{4,20},{8,24},{12,28},{16,0},{20,4},{24,8},{28,12},{1,17},{... | collective-permute-start | bytes 184328 | tf_op jit(solution)/shard_map/ppermute | solution.py:726
  85.7 2.3 %collective-permute-start.20 = (bf16[16,1280]{1,0:T(8,128)(2,1)S(1)}, bf16[16,1280]{1,0:T(8,128)(2,1)S(1)}, u32[]{:S(2)}, u32[]{:S(2)}) collective-permute-start(bf16[16,1280]{1,0:T(8,128)(2,1)S(1)} %get-tuple-element.208), channel_id=1, source_target_pairs={{0,16},{4,20},{8,24},{12,28},{16,0},{20,4},{24,8},{28,12},{1,17},{... | collective-permute-start | bytes 122888 | tf_op jit(solution)/shard_map/ppermute | solution.py:726
  88.0 2.2 %collective-permute-start.19 = (bf16[32,1920]{1,0:T(8,128)(2,1)S(1)}, bf16[32,1920]{1,0:T(8,128)(2,1)S(1)}, u32[]{:S(2)}, u32[]{:S(2)}) collective-permute-start(bf16[32,1920]{1,0:T(8,128)(2,1)S(1)} %pad_maximum_fusion.2), channel_id=1, source_target_pairs={{0,8},{4,12},{8,0},{12,4},{16,24},{20,28},{24,16},{28,20},{1,9},{5... | collective-permute-start | bytes 368648 | tf_op jit(solution)/shard_map/ppermute | solution.py:726
  90.9 2.2 %collective-permute-start.21 = (bf16[16,1152]{1,0:T(8,128)(2,1)S(1)}, bf16[16,1152]{1,0:T(8,128)(2,1)S(1)}, u32[]{:S(2)}, u32[]{:S(2)}) collective-permute-start(bf16[16,1152]{1,0:T(8,128)(2,1)S(1)} %add_convert_fusion.17), channel_id=1, source_target_pairs={{0,16},{4,20},{8,24},{12,28},{16,0},{20,4},{24,8},{28,12},{1,17},{... | collective-permute-start | bytes 110600 | tf_op jit(solution)/shard_map/ppermute | solution.py:726
  93.2 2.7 %collective-permute-done.21 = bf16[16,1152]{1,0:T(8,128)(2,1)S(1)} collective-permute-done((bf16[16,1152]{1,0:T(8,128)(2,1)S(1)}, bf16[16,1152]{1,0:T(8,128)(2,1)S(1)}, u32[]{:S(2)}, u32[]{:S(2)}) %collective-permute-start.21) | collective-permute-done | bytes 36896 | tf_op jit(solution)/shard_map/ppermute | solution.py:726
  95.9 1.9 %collective-permute-start.22 = (bf16[32,1152]{1,0:T(8,128)(2,1)S(1)}, bf16[32,1152]{1,0:T(8,128)(2,1)S(1)}, u32[]{:S(2)}, u32[]{:S(2)}) collective-permute-start(bf16[32,1152]{1,0:T(8,128)(2,1)S(1)} %pad_maximum_fusion.3), channel_id=1, source_target_pairs={{0,8},{4,12},{8,0},{12,4},{16,24},{20,28},{24,16},{28,20},{1,9},{5... | collective-permute-start | bytes 221192 | tf_op jit(solution)/shard_map/ppermute | solution.py:726
  106.3 2.5 %collective-permute-done.26 = f32[8,128]{1,0:T(8,128)S(1)} collective-permute-done((f32[8,128]{1,0:T(8,128)S(1)}, f32[8,128]{1,0:T(8,128)S(1)}, u32[]{:S(2)}, u32[]{:S(2)}) %collective-permute-start.26) | collective-permute-done | bytes 4128 | tf_op jit(solution)/shard_map/ppermute | solution.py:726
  108.9 3.8 %adam.1 = (f32[128,1536]{1,0:T(8,128)}, f32[128,512]{1,0:T(8,128)}, f32[128,512]{1,0:T(8,128)}, f32[128,512]{1,0:T(8,128)}, f32[9,128]{1,0:T(8,128)}, /*index=5*...) custom-call(s32[2]{0:T(128)S(1)} %pad_add_fusion.refs_0_.place, ...), custom_call_target="tpu_custom_call" | custom-call | tf_op jit(solution)/shard_map/adam/pallas_call | solution.py:713
  (107 shorter events, 26.8 us)
Async XLA Ops:
  2.6 8.7 %collective-permute-start.1 = (bf16[144,768]{1,0:T(8,128)(2,1)}, bf16[144,768]{1,0:T(8,128)(2,1)S(1)}, u32[]{:S(2)}, u32[]{:S(2)}) collective-permute-start(bf16[144,768]{1,0:T(8,128)(2,1)} %pack_first.1.refs_5_), channel_id=1, source_target_pairs={{0,2},{1,3},{2,0},{3,1},{4,6},{5,7},{6,4},{7,5},{8,10},{9,11},{10,... | collective-permute-start | bytes 663560 | tf_op jit(solution)/shard_map/ppermute | solution.py:726
  5.6 7.7 %collective-permute-start = (bf16[144,768]{1,0:T(8,128)(2,1)}, bf16[144,768]{1,0:T(8,128)(2,1)}, u32[]{:S(2)}, u32[]{:S(2)}) collective-permute-start(bf16[144,768]{1,0:T(8,128)(2,1)} %pack_first.1.refs_5_), channel_id=1, source_target_pairs={{0,1},{1,0},{2,3},{3,2},{4,5},{5,4},{6,7},{7,6},{8,9},{9,8},{10,11... | collective-permute-start | bytes 663560 | tf_op jit(solution)/shard_map/ppermute | solution.py:726
  11.3 9.4 %collective-permute-start.4 = (bf16[128,768]{1,0:T(8,128)(2,1)}, bf16[128,768]{1,0:T(8,128)(2,1)}, u32[]{:S(2)}, u32[]{:S(2)}) collective-permute-start(bf16[128,768]{1,0:T(8,128)(2,1)} %get-tuple-element.126.refs_5_), channel_id=1, source_target_pairs={{0,2},{1,3},{2,0},{3,1},{4,6},{5,7},{6,4},{7,5},{8,10},{9,11},{10,... | collective-permute-start | bytes 589832 | tf_op jit(solution)/shard_map/ppermute | solution.py:726
  13.0 15.3 %collective-permute-start.6 = (bf16[128,1536]{1,0:T(8,128)(2,1)}, bf16[128,1536]{1,0:T(8,128)(2,1)S(1)}, u32[]{:S(2)}, u32[]{:S(2)}) collective-permute-start(bf16[128,1536]{1,0:T(8,128)(2,1)} %get-tuple-element.130.refs_6_), channel_id=1, source_target_pairs={{0,2},{1,3},{2,0},{3,1},{4,6},{5,7},{6,4},{7,5},{8,10},{9,11},{10,... | collective-permute-start | bytes 1179656 | tf_op jit(solution)/shard_map/ppermute | solution.py:726
  13.3 8.0 %collective-permute-start.3 = (bf16[128,768]{1,0:T(8,128)(2,1)}, bf16[128,768]{1,0:T(8,128)(2,1)}, u32[]{:S(2)}, u32[]{:S(2)}) collective-permute-start(bf16[128,768]{1,0:T(8,128)(2,1)} %get-tuple-element.126.refs_5_), channel_id=1, source_target_pairs={{0,1},{1,0},{2,3},{3,2},{4,5},{5,4},{6,7},{7,6},{8,9},{9,8},{10,11... | collective-permute-start | bytes 589832 | tf_op jit(solution)/shard_map/ppermute | solution.py:726
  21.2 7.6 %collective-permute-start.7 = (bf16[128,1536]{1,0:T(8,128)(2,1)}, bf16[128,1536]{1,0:T(8,128)(2,1)S(1)}, u32[]{:S(2)}, u32[]{:S(2)}) collective-permute-start(bf16[128,1536]{1,0:T(8,128)(2,1)} %get-tuple-element.130.refs_6_), channel_id=1, source_target_pairs={{0,1},{1,0},{2,3},{3,2},{4,5},{5,4},{6,7},{7,6},{8,9},{9,8},{10,11... | collective-permute-start | bytes 1179656 | tf_op jit(solution)/shard_map/ppermute | solution.py:726
  49.0 14.2 %collective-permute-start.11 = (bf16[128,1920]{1,0:T(8,128)(2,1)S(1)}, bf16[128,1920]{1,0:T(8,128)(2,1)S(1)}, u32[]{:S(2)}, u32[]{:S(2)}) collective-permute-start(bf16[128,1920]{1,0:T(8,128)(2,1)S(1)} %get-tuple-element.196.refs_12_), channel_id=1, source_target_pairs={{0,2},{1,3},{2,0},{3,1},{4,6},{5,7},{6,4},{7,5},{8,10},{9,11},{10,... | collective-permute-start | bytes 1474568 | tf_op jit(solution)/shard_map/ppermute | solution.py:726
  63.3 8.4 %collective-permute-start.12 = (bf16[64,1920]{1,0:T(8,128)(2,1)S(1)}, bf16[64,1920]{1,0:T(8,128)(2,1)S(1)}, u32[]{:S(2)}, u32[]{:S(2)}) collective-permute-start(bf16[64,1920]{1,0:T(8,128)(2,1)S(1)} %get-tuple-element.200.refs_1_), channel_id=1, source_target_pairs={{0,4},{4,0},{8,12},{12,8},{16,20},{20,16},{24,28},{28,24},{1,5},{5... | collective-permute-start | bytes 737288 | tf_op jit(solution)/shard_map/ppermute | solution.py:726
  65.4 9.8 %collective-permute-start.14 = (bf16[128,1280]{1,0:T(8,128)(2,1)S(1)}, bf16[128,1280]{1,0:T(8,128)(2,1)S(1)}, u32[]{:S(2)}, u32[]{:S(2)}) collective-permute-start(bf16[128,1280]{1,0:T(8,128)(2,1)S(1)} %get-tuple-element.198.refs_0_), channel_id=1, source_target_pairs={{0,2},{1,3},{2,0},{3,1},{4,6},{5,7},{6,4},{7,5},{8,10},{9,11},{10,... | collective-permute-start | bytes 983048 | tf_op jit(solution)/shard_map/ppermute | solution.py:726
  71.9 5.0 %collective-permute-start.13 = (bf16[32,1920]{1,0:T(8,128)(2,1)S(1)}, bf16[32,1920]{1,0:T(8,128)(2,1)S(1)}, u32[]{:S(2)}, u32[]{:S(2)}) collective-permute-start(bf16[32,1920]{1,0:T(8,128)(2,1)S(1)} %get-tuple-element.203), channel_id=1, source_target_pairs={{0,8},{4,12},{8,0},{12,4},{16,24},{20,28},{24,16},{28,20},{1,9},{5... | collective-permute-start | bytes 368648 | tf_op jit(solution)/shard_map/ppermute | solution.py:726
  75.3 5.5 %collective-permute-start.16 = (bf16[64,1280]{1,0:T(8,128)(2,1)S(1)}, bf16[64,1280]{1,0:T(8,128)(2,1)S(1)}, u32[]{:S(2)}, u32[]{:S(2)}) collective-permute-start(bf16[64,1280]{1,0:T(8,128)(2,1)S(1)} %get-tuple-element.202), channel_id=1, source_target_pairs={{0,4},{4,0},{8,12},{12,8},{16,20},{20,16},{24,28},{28,24},{1,5},{5... | collective-permute-start | bytes 491528 | tf_op jit(solution)/shard_map/ppermute | solution.py:726
  77.0 5.5 %collective-permute-start.15 = (bf16[16,1920]{1,0:T(8,128)(2,1)S(1)}, bf16[16,1920]{1,0:T(8,128)(2,1)S(1)}, u32[]{:S(2)}, u32[]{:S(2)}) collective-permute-start(bf16[16,1920]{1,0:T(8,128)(2,1)S(1)} %add_convert_fusion.13), channel_id=1, source_target_pairs={{0,16},{4,20},{8,24},{12,28},{16,0},{20,4},{24,8},{28,12},{1,17},{... | collective-permute-start | bytes 184328 | tf_op jit(solution)/shard_map/ppermute | solution.py:726
  80.8 4.9 %collective-permute-start.18 = (bf16[32,1280]{1,0:T(8,128)(2,1)S(1)}, bf16[32,1280]{1,0:T(8,128)(2,1)S(1)}, u32[]{:S(2)}, u32[]{:S(2)}) collective-permute-start(bf16[32,1280]{1,0:T(8,128)(2,1)S(1)} %get-tuple-element.206), channel_id=1, source_target_pairs={{0,8},{4,12},{8,0},{12,4},{16,24},{20,28},{24,16},{28,20},{1,9},{5... | collective-permute-start | bytes 245768 | tf_op jit(solution)/shard_map/ppermute | solution.py:726
  82.5 5.5 %collective-permute-start.17 = (bf16[16,1920]{1,0:T(8,128)(2,1)S(1)}, bf16[16,1920]{1,0:T(8,128)(2,1)S(1)}, u32[]{:S(2)}, u32[]{:S(2)}) collective-permute-start(bf16[16,1920]{1,0:T(8,128)(2,1)S(1)} %add_convert_fusion.12), channel_id=1, source_target_pairs={{0,16},{4,20},{8,24},{12,28},{16,0},{20,4},{24,8},{28,12},{1,17},{... | collective-permute-start | bytes 184328 | tf_op jit(solution)/shard_map/ppermute | solution.py:726
  85.7 5.2 %collective-permute-start.20 = (bf16[16,1280]{1,0:T(8,128)(2,1)S(1)}, bf16[16,1280]{1,0:T(8,128)(2,1)S(1)}, u32[]{:S(2)}, u32[]{:S(2)}) collective-permute-start(bf16[16,1280]{1,0:T(8,128)(2,1)S(1)} %get-tuple-element.208), channel_id=1, source_target_pairs={{0,16},{4,20},{8,24},{12,28},{16,0},{20,4},{24,8},{28,12},{1,17},{... | collective-permute-start | bytes 122888 | tf_op jit(solution)/shard_map/ppermute | solution.py:726
  88.0 5.1 %collective-permute-start.19 = (bf16[32,1920]{1,0:T(8,128)(2,1)S(1)}, bf16[32,1920]{1,0:T(8,128)(2,1)S(1)}, u32[]{:S(2)}, u32[]{:S(2)}) collective-permute-start(bf16[32,1920]{1,0:T(8,128)(2,1)S(1)} %pad_maximum_fusion.2), channel_id=1, source_target_pairs={{0,8},{4,12},{8,0},{12,4},{16,24},{20,28},{24,16},{28,20},{1,9},{5... | collective-permute-start | bytes 368648 | tf_op jit(solution)/shard_map/ppermute | solution.py:726
  90.9 4.9 %collective-permute-start.21 = (bf16[16,1152]{1,0:T(8,128)(2,1)S(1)}, bf16[16,1152]{1,0:T(8,128)(2,1)S(1)}, u32[]{:S(2)}, u32[]{:S(2)}) collective-permute-start(bf16[16,1152]{1,0:T(8,128)(2,1)S(1)} %add_convert_fusion.17), channel_id=1, source_target_pairs={{0,16},{4,20},{8,24},{12,28},{16,0},{20,4},{24,8},{28,12},{1,17},{... | collective-permute-start | bytes 110600 | tf_op jit(solution)/shard_map/ppermute | solution.py:726
  95.9 4.4 %collective-permute-start.22 = (bf16[32,1152]{1,0:T(8,128)(2,1)S(1)}, bf16[32,1152]{1,0:T(8,128)(2,1)S(1)}, u32[]{:S(2)}, u32[]{:S(2)}) collective-permute-start(bf16[32,1152]{1,0:T(8,128)(2,1)S(1)} %pad_maximum_fusion.3), channel_id=1, source_target_pairs={{0,8},{4,12},{8,0},{12,4},{16,24},{20,28},{24,16},{28,20},{1,9},{5... | collective-permute-start | bytes 221192 | tf_op jit(solution)/shard_map/ppermute | solution.py:726
  97.7 11.0 %collective-permute-start.27 = (bf16[64,1920]{1,0:T(8,128)(2,1)S(1)}, bf16[64,1920]{1,0:T(8,128)(2,1)S(1)}, u32[]{:S(2)}, u32[]{:S(2)}) collective-permute-start(bf16[64,1920]{1,0:T(8,128)(2,1)S(1)} %pad_maximum_fusion.early.refs_0_), channel_id=1, source_target_pairs={{0,4},{4,0},{8,12},{12,8},{16,20},{20,16},{24,28},{28,24},{1,5},{5... | collective-permute-start | bytes 737288 | tf_op jit(solution)/shard_map/ppermute | solution.py:726
  101.0 3.4 %collective-permute-start.25 = (f32[8,128]{1,0:T(8,128)S(1)}, f32[8,128]{1,0:T(8,128)S(1)}, u32[]{:S(2)}, u32[]{:S(2)}) collective-permute-start(f32[8,128]{1,0:T(8,128)S(1)} %half_squares.1), channel_id=1, source_target_pairs={{0,3},{1,2},{2,1},{3,0},{4,7},{5,6},{6,5},{7,4},{8,11},{9,10},{10,... | collective-permute-start | bytes 12296 | tf_op jit(solution)/shard_map/ppermute | solution.py:726
  101.1 3.7 %collective-permute-start.24 = (f32[8,128]{1,0:T(8,128)S(1)}, f32[8,128]{1,0:T(8,128)S(1)}, u32[]{:S(2)}, u32[]{:S(2)}) collective-permute-start(f32[8,128]{1,0:T(8,128)S(1)} %half_squares.1), channel_id=1, source_target_pairs={{0,2},{1,3},{2,0},{3,1},{4,6},{5,7},{6,4},{7,5},{8,10},{9,11},{10,... | collective-permute-start | bytes 12296 | tf_op jit(solution)/shard_map/ppermute | solution.py:726
  101.5 3.2 %collective-permute-start.23 = (f32[8,128]{1,0:T(8,128)S(1)}, f32[8,128]{1,0:T(8,128)S(1)}, u32[]{:S(2)}, u32[]{:S(2)}) collective-permute-start(f32[8,128]{1,0:T(8,128)S(1)} %half_squares.1), channel_id=1, source_target_pairs={{0,1},{1,0},{2,3},{3,2},{4,5},{5,4},{6,7},{7,6},{8,9},{9,8},{10,11... | collective-permute-start | bytes 12296 | tf_op jit(solution)/shard_map/ppermute | solution.py:726
  102.9 5.9 %collective-permute-start.28 = (bf16[64,1152]{1,0:T(8,128)(2,1)S(1)}, bf16[64,1152]{1,0:T(8,128)(2,1)S(1)}, u32[]{:S(2)}, u32[]{:S(2)}) collective-permute-start(bf16[64,1152]{1,0:T(8,128)(2,1)S(1)} %pad_maximum_fusion.1.late.refs_2_), channel_id=1, source_target_pairs={{0,4},{4,0},{8,12},{12,8},{16,20},{20,16},{24,28},{28,24},{1,5},{5... | collective-permute-start | bytes 442376 | tf_op jit(solution)/shard_map/ppermute | solution.py:726
  104.8 4.0 %collective-permute-start.26 = (f32[8,128]{1,0:T(8,128)S(1)}, f32[8,128]{1,0:T(8,128)S(1)}, u32[]{:S(2)}, u32[]{:S(2)}) collective-permute-start(f32[8,128]{1,0:T(8,128)S(1)} %add_add_fusion), channel_id=1, source_target_pairs={{0,4},{4,0},{8,12},{12,8},{16,20},{20,16},{24,28},{28,24},{1,5},{5... | collective-permute-start | bytes 12296 | tf_op jit(solution)/shard_map/ppermute | solution.py:726
  (25 other events, 471.3 us)
